TPU v7x, 32 devices: a whole 2x2x4 slice. The times are simulated.
32 devices in a mesh: row: 8 (over z, y), col: 4 (over x, core).
Axes of the slice: x: 2, y: 2, z: 4, core: 2. Of those that a mesh axis runs over, the one named last changes fastest.
Arguments:
- acts: bfloat16 [16384, 4096], P('row', 'col'), may hold values from -6 to 6
- out_grads: bfloat16 [16384, 1, 4096], P('row', None, 'col'), may hold values from -0.0234375 to 0.0234375
- row_stat: float32 [1, 4096], P(None, 'row'), may hold values from 0.02 to 0.2
- col_stat: float32 [1, 4096], P(None, 'col'), may hold values from 0.02 to 0.2
- master: float32 [4096, 1, 4096], P('row', None, 'col'), may hold values from -0.09375 to 0.09375
Outputs:
- fresh_weights: bfloat16 [4096, 1, 4096], P(None, None, 'col')
- master_out: float32 [4096, 1, 4096], P('row', None, 'col')
- update_out: float32 [4096, 1, 4096], P('row', None, 'col')
- row_out: float32 [1, 4096], P(None, 'row')
- col_out: float32 [1, 4096], P(None, 'col')
All inputs are finite; a program needn't handle non-finite values.
Results may differ from a plain program's by a relative error of at most 0.001.
Values may be sent and summed in bfloat16 or wider, within the bound.
A program may use at most 256 MiB of HBM per device.

v0:
```python
import jax
import jax.numpy as jnp
from jax import lax
from jax.sharding import PartitionSpec as P

D = 4096


def contract_tokens(left, right):
    return lax.dot_general(
        left, right, (((0,), (0,)), ((), ())), preferred_element_type=jnp.float32
    )


def shards(acts, out_grads, row_stat, col_stat, master):
    acts_full = lax.all_gather(acts, "col", axis=1, tiled=True)
    tok_here, mats, width_c = out_grads.shape
    flat_out = out_grads.reshape(tok_here, mats * width_c)
    rows_here = master.shape[0]
    grad = lax.psum_scatter(
        contract_tokens(acts_full, flat_out), "row", scatter_dimension=0, tiled=True
    )
    grad = grad.reshape(rows_here, mats, width_c)
    squares = grad * grad + 1e-30
    row_part = jnp.sum(squares, axis=2).T
    col_part = jnp.sum(squares, axis=0)
    row_sum = lax.psum(row_part, "col")
    row_out = 0.75 * row_stat + 0.25 * row_sum / D
    col_sum, row_total = lax.psum((col_part, jnp.sum(row_out, axis=1)), "row")
    col_out = 0.75 * col_stat + 0.25 * col_sum / D
    row_mean = row_total / D
    raw = grad * lax.rsqrt(row_out.T[:, :, None] * col_out[None, :, :] / row_mean[None, :, None])
    total_sq = lax.psum(jnp.sum(raw * raw, axis=(0, 2)), ("row", "col"))
    rms = jnp.sqrt(total_sq / (D * D))
    update_out = raw / jnp.maximum(1.0, rms)[None, :, None]
    master_out = master - 0.01 * update_out
    fresh = lax.all_gather(master_out.astype(jnp.bfloat16), "row", axis=0, tiled=True)
    return (fresh, master_out, update_out, row_out, col_out)


def solution(mesh):
    in_specs = (
        P("row", "col"),
        P("row", None, "col"),
        P(None, "row"),
        P(None, "col"),
        P("row", None, "col"),
    )
    out_specs = (
        P(None, None, "col"),
        P("row", None, "col"),
        P("row", None, "col"),
        P(None, "row"),
        P(None, "col"),
    )
    return jax.shard_map(shards, mesh=mesh, in_specs=in_specs, out_specs=out_specs, check_vma=False)
```

profile of v0, /device:TPU:0, one launch (start us, length us, event | category | flops | bytes accessed | tf_op | source)
XLA Modules:
  0.0 638.2 jit_solution(18011767510570468994)
XLA Ops:
  7.2 0.0 all-gather.3.cloned.1.call-start
  7.2 0.7 all-gather.3.cloned.1.call-update
  7.9 0.0 reduce-scatter.2.cloned.1.call-start
  7.9 110.3 %all-gather.3.cloned.1.call-done = bf16[2048,4096]{1,0:T(8,128)(2,1)} async-done(((bf16[2048,1024]{1,0:T(8,128)(2,1)}), bf16[2048,4096]{1,0:T(8,128)(2,1)}) %all-gather.3.cloned.1.call-update) | async-done | bytes 16777232 | tf_op jit(solution)/shard_map/all_gather | solution.py:16
  118.2 23.8 %fusion = f32[4096,1024]{1,0:T(8,128)} fusion(bf16[2048,4096]{1,0:T(8,128)(2,1)} %all-gather.3.cloned.1.call-done, bf16[2048,1,1024]{2,0,1:T(8,128)(2,1)} %param.6), kind=kOutput, calls=%fused_computation | convolution fusion | flops 17179869184 | bytes 37748736 | tf_op jit(solution)/shard_map/dot_general | solution.py:10
  142.0 0.0 reduce-scatter.2.cloned.1.call-update
  142.0 0.0 copy-start.5
  142.0 0.0 copy-start.4
  142.0 0.0 all-gather.5.cloned.1.call-start
  142.1 282.1 %reduce-scatter.2.cloned.1.call-done = f32[512,1024]{1,0:T(8,128)} async-done(((f32[4096,1024]{1,0:T(8,128)}), f32[512,1024]{1,0:T(8,128)}) %reduce-scatter.2.cloned.1.call-update) | async-done | bytes 2097168 | tf_op jit(solution)/shard_map/reduce_scatter | solution.py:20
  424.1 2.1 fusion.2
  426.3 6.8 %psum.28 = f32[1,512]{1,0:T(1,128)S(1)} all-reduce(f32[1,512]{1,0:T(1,128)S(1)} %bitcast.24), channel_id=1, replica_groups=mesh['row'=8,'col'=4] {'col'}, use_global_device_ids=true, to_apply=%region_2.0 | all-reduce | flops 512 | bytes 4096 | tf_op jit(solution)/shard_map/psum | solution.py:27
  433.1 0.6 fusion.6
  433.7 20.4 %all-reduce = (f32[1]{0:T(128)}, f32[1,1024]{1,0:T(1,128)S(1)}) all-reduce(f32[1]{0:T(128)} %bitcast.5, f32[1,1024]{1,0:T(1,128)S(1)} %bitcast.23), channel_id=1, replica_groups=mesh['row'=8,'col'=4] {'row'}, use_global_device_ids=true, to_apply=%region_6.0 | all-reduce | flops 1025 | bytes 8200 | tf_op jit(solution)/shard_map/psum | solution.py:29
  454.8 0.0 copy-start.2
  454.8 1.5 multiply_reduce_fusion
  456.3 37.2 %psum.31 = f32[1]{0:T(128)} all-reduce(f32[1]{0:T(128)} %bitcast.7), channel_id=1, replica_groups=mesh['row'=8,'col'=4] {'row','col'}, use_global_device_ids=true, to_apply=%region_8.0 | all-reduce | flops 1 | bytes 8 | tf_op jit(solution)/shard_map/psum | solution.py:33
  494.3 3.9 fusion.5
  498.2 0.0 all-gather.5.cloned.1.call-update
  498.2 0.4 fusion.4
  498.7 3.5 copy.12
  502.1 3.5 copy.11
  505.6 118.3 %all-gather.5.cloned.1.call-done = bf16[4096,1,1024]{2,0,1:T(8,128)(2,1)} async-done(((bf16[512,1,1024]{2,0,1:T(8,128)(2,1)}), bf16[4096,1,1024]{2,0,1:T(8,128)(2,1)}) %all-gather.5.cloned.1.call-update) | async-done | bytes 8388624 | tf_op jit(solution)/shard_map/all_gather | solution.py:37
  623.9 7.8 %copy.16 = bf16[4096,1,1024]{2,0,1:T(8,128)(2,1)} copy(bf16[4096,1,1024]{2,0,1:T(8,128)(2,1)} %all-gather.5.cloned.1.call-done) | data formatting | bytes 16777216
  (10 shorter events, 0.0 us)
Async XLA Ops:
  7.2 111.0 %all-gather.3.cloned.1.call-start = ((), (), s32[]{:S(2)}) async-start(), calls=%async_computation.1 | async-start | bytes 20971520 | tf_op jit(solution)/shard_map/all_gather | solution.py:16
  7.9 416.2 %reduce-scatter.2.cloned.1.call-start = ((), (), s32[]{:S(2)}) async-start(), calls=%async_computation.2 | async-start | bytes 18874368 | tf_op jit(solution)/shard_map/reduce_scatter | solution.py:20
  142.0 291.1 %copy-start.5 = (f32[1,512]{1,0:T(1,128)S(1)}, f32[1,512]{1,0:T(1,128)}, u32[]{:S(2)}) copy-start(f32[1,512]{1,0:T(1,128)} %param.7) | copy-start | bytes 6148
  142.0 312.8 %copy-start.4 = (f32[1,1024]{1,0:T(1,128)S(1)}, f32[1,1024]{1,0:T(1,128)}, u32[]{:S(2)}) copy-start(f32[1,1024]{1,0:T(1,128)} %param.8) | copy-start | bytes 12292
  142.0 481.9 %all-gather.5.cloned.1.call-start = ((), (), s32[]{:S(2)}) async-start(), calls=%async_computation.3 | async-start | bytes 9437184 | tf_op jit(solution)/shard_map/all_gather | solution.py:37
  424.1 30.7 %copy-start = (f32[512,1024]{1,0:T(8,128)S(1)}, f32[512,1024]{1,0:T(8,128)}, u32[]{:S(2)}) copy-start(f32[512,1024]{1,0:T(8,128)} %reduce-scatter.2.cloned.1.call-done) | copy-start | bytes 6291460
  433.7 64.5 %copy-start.3 = (f32[1,512]{1,0:T(1,128)}, f32[1,512]{1,0:T(1,128)S(1)}, u32[]{:S(2)}) copy-start(f32[1,512]{1,0:T(1,128)S(1)} %get-tuple-element.26) | copy-start | bytes 6148
  454.8 43.4 %copy-start.2 = (f32[1,1024]{1,0:T(1,128)}, f32[1,1024]{1,0:T(1,128)S(1)}, u32[]{:S(2)}) copy-start(f32[1,1024]{1,0:T(1,128)S(1)} %multiply_add_fusion.1) | copy-start | bytes 12292
  498.6 3.5 copy-start.1
Sparse Core Ops, SparseCore 0:
  9.6 108.6 all-gather.2
  142.1 281.9 reduce-scatter.1
  498.3 125.5 all-gather.4
where the time goes:
time: 639 us; the launch traced here: 638 us
  waiting for transfers between devices  511 us (80%)
  blocking collectives  64.5 us (10%)
  matrix products  23.8 us (4%)
  between operations  15.2 us (2%)
  local copies, waits for them, and re-layouts  14.7 us (2%)
  other arithmetic  8.6 us (1%)
    reduce_scatter x1, waiting for transfers between devices, shards(): lax.psum_scatter(contract_tokens(acts_full, flat_out), 'row', scatter_dim...  282 us
    all_gather x1, waiting for transfers between devices, shards(): lax.all_gather(master_out.astype(jnp.bfloat16), 'row', axis=0, tiled=True)  118 us
    all_gather x1, waiting for transfers between devices, shards(): acts_full = lax.all_gather(acts, 'col', axis=1, tiled=True)  110 us
    psum x1, blocking collectives, shards(): total_sq = lax.psum(jnp.sum(raw * raw, axis=(0, 2)), ('row', 'col'))  37.2 us
    dot_general x1, matrix products, contract_tokens(): lax.dot_general(left, right, (((0,), (0,)), ((), ())), preferred_element_...  23.8 us
    psum x1, blocking collectives, shards(): col_sum, row_total = lax.psum((col_part, jnp.sum(row_out, axis=1)), 'row')  20.4 us
    unnamed x15, local copies, waits for them, and re-layouts  14.7 us
  transfers between devices with their start and end apart: 3, of which 3 were waited for; matrix products, arithmetic and copies ran while one was open for 1% of the time, Pallas kernels for 0%

commit v1 on v0

--- a/solution.py
+++ b/solution.py
@@ -12,14 +12,59 @@
     )
 
 
+def pair_sum(part, axis, partner_bit, mine, scale):
+    n = lax.axis_size("row")
+    keep = lax.dynamic_index_in_dim(part, mine, axis, keepdims=False)
+    give = lax.dynamic_index_in_dim(part, 1 - mine, axis, keepdims=False)
+    got = lax.ppermute(
+        (give * scale).astype(jnp.float16), "row", [(r, r ^ partner_bit) for r in range(n)]
+    )
+    return keep + got.astype(jnp.float32) / scale
+
+
+def reduce_blocks(part, r, y_first, scale):
+    y, z_lo, z_hi = r % 2, (r // 2) % 2, r // 4
+    if y_first:
+        part = pair_sum(part, 2, 1, y, scale)
+        part = pair_sum(part, 1, 2, z_lo, scale)
+        return pair_sum(part, 0, 4, z_hi, scale)
+    part = pair_sum(part, 1, 2, z_lo, scale)
+    part = pair_sum(part, 0, 4, z_hi, scale)
+    return pair_sum(part, 0, 1, y, scale)
+
+
+def gradient_rows(acts, flat_out):
+    tok, width = acts.shape
+    cols = flat_out.shape[1]
+    r = lax.axis_index("row")
+    top = lax.pmax(jnp.max(jnp.abs(flat_out)).astype(jnp.float32), "row")
+    scale = 16384.0 / (6.0 * tok * lax.axis_size("row") * jnp.maximum(top, 1e-30))
+    step = width // 4
+    pieces = []
+    for k in range(2):
+        mine = acts.reshape(tok, 2, 2, step)[:, :, k].reshape(tok, 2 * step)
+        full = lax.all_gather(mine, "col", axis=1, tiled=True)
+        half = cols // 2
+        sums = []
+        for j in range(2):
+            part = contract_tokens(full, flat_out[:, j * half : (j + 1) * half])
+            part = part.reshape(2, 2, 2, step, half)
+            sums.append(reduce_blocks(part, r, j == 0, scale))
+        pieces.append(jnp.concatenate(sums, axis=1))
+    return jnp.concatenate(pieces, axis=0)
+
+
 def shards(acts, out_grads, row_stat, col_stat, master):
-    acts_full = lax.all_gather(acts, "col", axis=1, tiled=True)
     tok_here, mats, width_c = out_grads.shape
     flat_out = out_grads.reshape(tok_here, mats * width_c)
     rows_here = master.shape[0]
-    grad = lax.psum_scatter(
-        contract_tokens(acts_full, flat_out), "row", scatter_dimension=0, tiled=True
-    )
+    if (lax.axis_size("row"), lax.axis_size("col")) == (8, 4):
+        grad = gradient_rows(acts, flat_out)
+    else:
+        acts_full = lax.all_gather(acts, "col", axis=1, tiled=True)
+        grad = lax.psum_scatter(
+            contract_tokens(acts_full, flat_out), "row", scatter_dimension=0, tiled=True
+        )
     grad = grad.reshape(rows_here, mats, width_c)
     squares = grad * grad + 1e-30
     row_part = jnp.sum(squares, axis=2).T

time: 639 us -> 462 us (0.72)
  waiting for transfers between devices: 511 us -> 259 us
  starting transfers between devices: 0.12 us -> 27.1 us
  blocking collectives: 64.5 us -> 86.4 us
  local copies, waits for them, and re-layouts: 14.7 us -> 31.5 us
  other arithmetic: 8.6 us -> 16.9 us
    reduce_scatter x1 -> x0, waiting for transfers between devices: 282 us -> none  [shards(): lax.psum_scatter(contract_tokens(acts_full, flat_out), 'row', scatter_dim...]
    ppermute x0 -> x12, waiting for transfers between devices: none -> 67.3 us  [pair_sum(): lax.ppermute((give * scale).astype(jnp.float16), 'row', [(r, r ^ partner_...]
    all_gather x1 -> x2, waiting for transfers between devices: 110 us -> 73 us  [gradient_rows(): full = lax.all_gather(mine, 'col', axis=1, tiled=True)]
    ppermute x0 -> x12, starting transfers between devices: none -> 27 us  [pair_sum(): lax.ppermute((give * scale).astype(jnp.float16), 'row', [(r, r ^ partner_...]
    pmax x0 -> x1, blocking collectives: none -> 23.7 us  [gradient_rows(): top = lax.pmax(jnp.max(jnp.abs(flat_out)).astype(jnp.float32), 'row')]
    unnamed x15 -> x30, local copies, waits for them, and re-layouts: 14.7 us -> 26.7 us
    dot_general x1 -> x4, matrix products: 23.8 us -> 24.6 us  [contract_tokens(): lax.dot_general(left, right, (((0,), (0,)), ((), ())), preferred_element_...]
  transfers between devices with their start and end apart: 3 -> 15, of which waited for: 3 -> 9; matrix products, arithmetic and copies ran while one was open for 1% -> 9% of each run, Pallas kernels for 0% -> 0%
where the time goes in v1:
time: 462 us
  waiting for transfers between devices  259 us (56%)
  blocking collectives  86.4 us (19%)
  local copies, waits for them, and re-layouts  31.5 us (7%)
  starting transfers between devices  27.1 us (6%)
  matrix products  24.6 us (5%)
  other arithmetic  16.9 us (4%)
  between operations  16.1 us (3%)
    all_gather x1, waiting for transfers between devices, shards(): lax.all_gather(master_out.astype(jnp.bfloat16), 'row', axis=0, tiled=True)  118 us
    all_gather x2, waiting for transfers between devices, gradient_rows(): full = lax.all_gather(mine, 'col', axis=1, tiled=True)  73 us
    ppermute x12, waiting for transfers between devices, pair_sum(): lax.ppermute((give * scale).astype(jnp.float16), 'row', [(r, r ^ partner_...  67.3 us
    psum x1, blocking collectives, shards(): total_sq = lax.psum(jnp.sum(raw * raw, axis=(0, 2)), ('row', 'col'))  37.3 us
    ppermute x12, starting transfers between devices, pair_sum(): lax.ppermute((give * scale).astype(jnp.float16), 'row', [(r, r ^ partner_...  27 us
    unnamed x30, local copies, waits for them, and re-layouts  26.7 us
    dot_general x4, matrix products, contract_tokens(): lax.dot_general(left, right, (((0,), (0,)), ((), ())), preferred_element_...  24.6 us
    pmax x1, blocking collectives, gradient_rows(): top = lax.pmax(jnp.max(jnp.abs(flat_out)).astype(jnp.float32), 'row')  23.7 us
  transfers between devices with their start and end apart: 15, of which 9 were waited for; matrix products, arithmetic and copies ran while one was open for 9% of the time, Pallas kernels for 0%

profile of v1, /device:TPU:0, one launch (start us, length us, event | category | flops | bytes accessed | tf_op | source)
XLA Modules:
  0.0 461.5 jit_solution(8055281894921363803)
XLA Ops:
  7.2 6.4 %copy.35 = bf16[2048,1024]{0,1:T(8,128)(2,1)} copy(bf16[2048,1024]{1,0:T(8,128)(2,1)} %param.5) | data formatting | bytes 8388608 | tf_op args[0]
  13.6 4.8 %fusion.30 = (bf16[2048,2,1,256]{0,3,2,1:T(8,128)(2,1)}, bf16[2048,2,1,256]{0,3,2,1:T(8,128)(2,1)}) fusion(bf16[2048,2,2,256]{0,3,2,1:T(8,128)(2,1)} %bitcast.109), kind=kLoop, calls=%fused_computation.65 | loop fusion | bytes 8388608 | tf_op jit(solution)/shard_map/slice | solution.py:45
  19.3 3.8 abs_reduce_fusion
  23.0 23.7 %pmax.7 = f32[]{:T(128)} all-reduce(bf16[]{:T(256)} %abs_reduce_fusion), channel_id=1, replica_groups=mesh['row'=8,'col'=4] {'row'}, use_global_device_ids=true, to_apply=%region_1.0 | all-reduce | flops 1 | bytes 6 | tf_op jit(solution)/shard_map/pmax | solution.py:40
  47.5 32.1 %all-gather.4.cloned.1.call-done = bf16[2048,2048]{0,1:T(8,128)(2,1)} async-done(((bf16[2048,512]{0,1:T(8,128)(2,1)}), bf16[2048,2048]{0,1:T(8,128)(2,1)}) %all-gather.4.cloned.1.call-update) | async-done | bytes 8388624 | tf_op jit(solution)/shard_map/all_gather | solution.py:46
  79.6 7.7 %fusion.12 = f32[2048,512]{1,0:T(8,128)S(1)} fusion(bf16[2048,2048]{0,1:T(8,128)(2,1)} %all-gather.4.cloned.1.call-done, bf16[2048,1024]{1,0:T(8,128)(2,1)} %bitcast.112), kind=kOutput, calls=%fused_computation.26 | convolution fusion | flops 4294967296 | bytes 14680064 | tf_op jit(solution)/shard_map/dot_general | solution.py:10
  90.8 4.5 fusion.8
  99.2 40.9 %all-gather.6.cloned.1.call-done = bf16[2048,2048]{0,1:T(8,128)(2,1)} async-done(((bf16[2048,512]{0,1:T(8,128)(2,1)}), bf16[2048,2048]{0,1:T(8,128)(2,1)}) %all-gather.6.cloned.1.call-update) | async-done | bytes 8388624 | tf_op jit(solution)/shard_map/all_gather | solution.py:46
  140.1 7.8 %fusion.10 = f32[2048,512]{1,0:T(8,128)S(1)} fusion(bf16[2048,2048]{0,1:T(8,128)(2,1)} %all-gather.6.cloned.1.call-done, bf16[2048,1024]{1,0:T(8,128)(2,1)} %bitcast.113), kind=kOutput, calls=%fused_computation.24 | convolution fusion | flops 4294967296 | bytes 14680064 | tf_op jit(solution)/shard_map/dot_general | solution.py:10
  149.8 4.5 fusion.6
  161.7 11.9 %collective-permute-done.6 = f16[2,2,256,512]{3,2,1,0:T(8,128)(2,1)S(1)} collective-permute-done((f16[2,2,256,512]{3,2,1,0:T(8,128)(2,1)S(1)}, f16[2,2,256,512]{3,2,1,0:T(8,128)(2,1)S(1)}, u32[]{:S(2)}, u32[]{:S(2)}) %collective-permute-start.6) | collective-permute-done | bytes 1048608 | tf_op jit(solution)/shard_map/ppermute | solution.py:19
  175.7 16.3 %collective-permute-done.9 = f16[2,2,256,512]{3,2,1,0:T(8,128)(2,1)S(1)} collective-permute-done((f16[2,2,256,512]{3,2,1,0:T(8,128)(2,1)S(1)}, f16[2,2,256,512]{3,2,1,0:T(8,128)(2,1)S(1)}, u32[]{:S(2)}, u32[]{:S(2)}) %collective-permute-start.9) | collective-permute-done | bytes 1048608 | tf_op jit(solution)/shard_map/ppermute | solution.py:19
  194.0 9.4 %collective-permute-done.1 = f16[2,256,512]{2,1,0:T(8,128)(2,1)S(1)} collective-permute-done((f16[2,256,512]{2,1,0:T(8,128)(2,1)S(1)}, f16[2,256,512]{2,1,0:T(8,128)(2,1)S(1)}, u32[]{:S(2)}, u32[]{:S(2)}) %collective-permute-start.1) | collective-permute-done | bytes 524320 | tf_op jit(solution)/shard_map/ppermute | solution.py:19
  203.6 12.0 %collective-permute-start.2 = (f16[256,512]{1,0:T(8,128)(2,1)S(1)}, f16[256,512]{1,0:T(8,128)(2,1)S(1)}, u32[]{:S(2)}, u32[]{:S(2)}) collective-permute-start(f16[256,512]{1,0:T(8,128)(2,1)S(1)} %fusion.24), channel_id=1, source_target_pairs={{0,16},{4,20},{8,24},{12,28},{16,0},{20,4},{24,8},{28,12},{1,17},{... | collective-permute-start | bytes 786440 | tf_op jit(solution)/shard_map/ppermute | solution.py:19
  216.6 8.2 %collective-permute-done.7 = f16[2,256,512]{2,1,0:T(8,128)(2,1)S(1)} collective-permute-done((f16[2,256,512]{2,1,0:T(8,128)(2,1)S(1)}, f16[2,256,512]{2,1,0:T(8,128)(2,1)S(1)}, u32[]{:S(2)}, u32[]{:S(2)}) %collective-permute-start.7) | collective-permute-done | bytes 524320 | tf_op jit(solution)/shard_map/ppermute | solution.py:19
  227.4 16.2 %collective-permute-done.2 = f16[256,512]{1,0:T(8,128)(2,1)S(1)} collective-permute-done((f16[256,512]{1,0:T(8,128)(2,1)S(1)}, f16[256,512]{1,0:T(8,128)(2,1)S(1)}, u32[]{:S(2)}, u32[]{:S(2)}) %collective-permute-start.2) | collective-permute-done | bytes 262176 | tf_op jit(solution)/shard_map/ppermute | solution.py:19
  243.9 5.2 %collective-permute-done.8 = f16[256,512]{1,0:T(8,128)(2,1)S(1)} collective-permute-done((f16[256,512]{1,0:T(8,128)(2,1)S(1)}, f16[256,512]{1,0:T(8,128)(2,1)S(1)}, u32[]{:S(2)}, u32[]{:S(2)}) %collective-permute-start.8) | collective-permute-done | bytes 262176 | tf_op jit(solution)/shard_map/ppermute | solution.py:19
  249.8 5.9 %psum.28 = f32[1,512]{1,0:T(1,128)S(1)} all-reduce(f32[1,512]{1,0:T(1,128)S(1)} %bitcast.129), channel_id=1, replica_groups=mesh['row'=8,'col'=4] {'col'}, use_global_device_ids=true, to_apply=%region_3.4 | all-reduce | flops 512 | bytes 4096 | tf_op jit(solution)/shard_map/psum | solution.py:72
  256.3 19.5 %all-reduce = (f32[1]{0:T(128)}, f32[1,1024]{1,0:T(1,128)S(1)}) all-reduce(f32[1]{0:T(128)} %bitcast.40, f32[1,1024]{1,0:T(1,128)S(1)} %bitcast.128), channel_id=1, replica_groups=mesh['row'=8,'col'=4] {'row'}, use_global_device_ids=true, to_apply=%region_7.8 | all-reduce | flops 1025 | bytes 8200 | tf_op jit(solution)/shard_map/psum | solution.py:74
  277.9 37.3 %psum.31 = f32[1]{0:T(128)} all-reduce(f32[1]{0:T(128)} %bitcast.42), channel_id=1, replica_groups=mesh['row'=8,'col'=4] {'row','col'}, use_global_device_ids=true, to_apply=%region_9.10 | all-reduce | flops 1 | bytes 8 | tf_op jit(solution)/shard_map/psum | solution.py:78
  315.9 4.7 %fusion.28 = (bf16[512,1,1024]{2,0,1:T(8,128)(2,1)}, f32[512,1,1024]{2,0,1:T(8,128)}, f32[512,1,1024]{2,0,1:T(8,128)}) fusion(f32[512,1,1024]{2,1,0:T(1,128)} %param.9, f32[]{:T(128)} %bitcast.43, f32[]{:T(128)} %bitcast.41, f32[1024]{0:T(1024)S(1)} %bitcast.125, f32[512]{0:T(512)S(1)} %bitcast.127, f32[256,1,1024]{2,0,1:T(8,128)S(1)} %maximum_bitcast_fusion.1, ...), kind=kLoop, calls=%fused_computation.63 | loop fusion | flops 4194304 | bytes 9443336 | tf_op jit(solution)/shard_map/convert_element_type | solution.py:82
  320.7 5.2 %copy.43 = f32[512,1,1024]{2,1,0:T(1,128)} copy(f32[512,1,1024]{2,0,1:T(8,128)} %get-tuple-element.30) | data formatting | bytes 4194304
  329.4 117.9 %all-gather.8.cloned.1.call-done = bf16[4096,1,1024]{2,0,1:T(8,128)(2,1)} async-done(((bf16[512,1,1024]{2,0,1:T(8,128)(2,1)}), bf16[4096,1,1024]{2,0,1:T(8,128)(2,1)}) %all-gather.8.cloned.1.call-update) | async-done | bytes 8388624 | tf_op jit(solution)/shard_map/all_gather | solution.py:82
  447.2 7.8 %copy.52 = bf16[4096,1,1024]{2,0,1:T(8,128)(2,1)} copy(bf16[4096,1,1024]{2,0,1:T(8,128)(2,1)} %all-gather.8.cloned.1.call-done) | data formatting | bytes 16777216
  (80 shorter events, 31.5 us)
Async XLA Ops:
  7.2 72.5 %all-gather.4.cloned.1.call-start = ((), (), s32[]{:S(2)}) async-start(), calls=%async_computation | async-start | bytes 10485760 | tf_op jit(solution)/shard_map/all_gather | solution.py:46
  18.5 121.6 %all-gather.6.cloned.1.call-start = ((), (), s32[]{:S(2)}) async-start(), calls=%async_computation.1 | async-start | bytes 10485760 | tf_op jit(solution)/shard_map/all_gather | solution.py:46
  19.2 428.0 %all-gather.8.cloned.1.call-start = ((), (), s32[]{:S(2)}) async-start(), calls=%async_computation.2 | async-start | bytes 9437184 | tf_op jit(solution)/shard_map/all_gather | solution.py:82
  79.6 11.2 %copy-start.1 = (bf16[2048,1,1024]{2,0,1:T(8,128)(2,1)S(1)}, bf16[2048,1,1024]{2,0,1:T(8,128)(2,1)}, u32[]{:S(2)}) copy-start(bf16[2048,1,1024]{2,0,1:T(8,128)(2,1)} %param.6) | copy-start | bytes 12582916
  79.6 11.2 %copy-start.12 = (bf16[2048,2048]{0,1:T(8,128)(2,1)S(1)}, bf16[2048,2048]{0,1:T(8,128)(2,1)}, u32[]{:S(2)}) copy-start(bf16[2048,2048]{0,1:T(8,128)(2,1)} %all-gather.4.cloned.1.call-done) | copy-start | bytes 25165828
  89.3 66.8 %collective-permute-start = (f16[2,2,256,512]{3,2,1,0:T(8,128)(2,1)S(1)}, f16[2,2,256,512]{3,2,1,0:T(8,128)(2,1)}, u32[]{:S(2)}, u32[]{:S(2)}) collective-permute-start(f16[2,2,256,512]{3,2,1,0:T(8,128)(2,1)S(1)} %fusion.14), channel_id=1, source_target_pairs={{0,4},{4,0},{8,12},{12,8},{16,20},{20,16},{24,28},{28,24},{1,5},{5... | collective-permute-start | bytes 3145736 | tf_op jit(solution)/shard_map/ppermute | solution.py:19
  97.6 61.0 %collective-permute-start.3 = (f16[2,2,256,512]{3,2,1,0:T(8,128)(2,1)S(1)}, f16[2,2,256,512]{3,2,1,0:T(8,128)(2,1)S(1)}, u32[]{:S(2)}, u32[]{:S(2)}) collective-permute-start(f16[2,2,256,512]{3,2,1,0:T(8,128)(2,1)S(1)} %fusion.15), channel_id=1, source_target_pairs={{0,8},{4,12},{8,0},{12,4},{16,24},{20,28},{24,16},{28,20},{1,9},{5... | collective-permute-start | bytes 3145736 | tf_op jit(solution)/shard_map/ppermute | solution.py:19
  140.1 9.7 %copy-start.2 = (bf16[2048,1,1024]{2,0,1:T(8,128)(2,1)S(1)}, bf16[2048,1,1024]{2,0,1:T(8,128)(2,1)}, u32[]{:S(2)}) copy-start(bf16[2048,1,1024]{2,0,1:T(8,128)(2,1)} %param.6) | copy-start | bytes 12582916
  140.1 9.7 %copy-start.11 = (bf16[2048,2048]{0,1:T(8,128)(2,1)S(1)}, bf16[2048,2048]{0,1:T(8,128)(2,1)}, u32[]{:S(2)}) copy-start(bf16[2048,2048]{0,1:T(8,128)(2,1)} %all-gather.6.cloned.1.call-done) | copy-start | bytes 25165828
  148.2 25.4 %collective-permute-start.6 = (f16[2,2,256,512]{3,2,1,0:T(8,128)(2,1)S(1)}, f16[2,2,256,512]{3,2,1,0:T(8,128)(2,1)S(1)}, u32[]{:S(2)}, u32[]{:S(2)}) collective-permute-start(f16[2,2,256,512]{3,2,1,0:T(8,128)(2,1)S(1)} %fusion.16), channel_id=1, source_target_pairs={{0,4},{4,0},{8,12},{12,8},{16,20},{20,16},{24,28},{28,24},{1,5},{5... | collective-permute-start | bytes 3145736 | tf_op jit(solution)/shard_map/ppermute | solution.py:19
  149.8 6.4 %copy-start.6 = (f32[2048,512]{1,0:T(8,128)S(1)}, f32[2048,512]{1,0:T(8,128)}, u32[]{:S(2)}) copy-start(f32[2048,512]{1,0:T(8,128)} %copy-done.5) | copy-start | bytes 12582916
  154.6 37.3 %collective-permute-start.9 = (f16[2,2,256,512]{3,2,1,0:T(8,128)(2,1)S(1)}, f16[2,2,256,512]{3,2,1,0:T(8,128)(2,1)S(1)}, u32[]{:S(2)}, u32[]{:S(2)}) collective-permute-start(f16[2,2,256,512]{3,2,1,0:T(8,128)(2,1)S(1)} %fusion.17), channel_id=1, source_target_pairs={{0,8},{4,12},{8,0},{12,4},{16,24},{20,28},{24,16},{28,20},{1,9},{5... | collective-permute-start | bytes 3145736 | tf_op jit(solution)/shard_map/ppermute | solution.py:19
  158.0 45.3 %collective-permute-start.1 = (f16[2,256,512]{2,1,0:T(8,128)(2,1)S(1)}, f16[2,256,512]{2,1,0:T(8,128)(2,1)S(1)}, u32[]{:S(2)}, u32[]{:S(2)}) collective-permute-start(f16[2,256,512]{2,1,0:T(8,128)(2,1)S(1)} %fusion.22), channel_id=1, source_target_pairs={{0,8},{4,12},{8,0},{12,4},{16,24},{20,28},{24,16},{28,20},{1,9},{5... | collective-permute-start | bytes 1572872 | tf_op jit(solution)/shard_map/ppermute | solution.py:19
  159.2 56.4 %collective-permute-start.4 = (f16[2,256,512]{2,1,0:T(8,128)(2,1)S(1)}, f16[2,256,512]{2,1,0:T(8,128)(2,1)S(1)}, u32[]{:S(2)}, u32[]{:S(2)}) collective-permute-start(f16[2,256,512]{2,1,0:T(8,128)(2,1)S(1)} %fusion.20), channel_id=1, source_target_pairs={{0,16},{4,20},{8,24},{12,28},{16,0},{20,4},{24,8},{28,12},{1,17},{... | collective-permute-start | bytes 1572872 | tf_op jit(solution)/shard_map/ppermute | solution.py:19
  174.1 50.7 %collective-permute-start.7 = (f16[2,256,512]{2,1,0:T(8,128)(2,1)S(1)}, f16[2,256,512]{2,1,0:T(8,128)(2,1)S(1)}, u32[]{:S(2)}, u32[]{:S(2)}) collective-permute-start(f16[2,256,512]{2,1,0:T(8,128)(2,1)S(1)} %fusion.23), channel_id=1, source_target_pairs={{0,8},{4,12},{8,0},{12,4},{16,24},{20,28},{24,16},{28,20},{1,9},{5... | collective-permute-start | bytes 1572872 | tf_op jit(solution)/shard_map/ppermute | solution.py:19
  192.5 34.0 %collective-permute-start.10 = (f16[2,256,512]{2,1,0:T(8,128)(2,1)S(1)}, f16[2,256,512]{2,1,0:T(8,128)(2,1)S(1)}, u32[]{:S(2)}, u32[]{:S(2)}) collective-permute-start(f16[2,256,512]{2,1,0:T(8,128)(2,1)S(1)} %fusion.21), channel_id=1, source_target_pairs={{0,16},{4,20},{8,24},{12,28},{16,0},{20,4},{24,8},{28,12},{1,17},{... | collective-permute-start | bytes 1572872 | tf_op jit(solution)/shard_map/ppermute | solution.py:19
  203.6 40.0 %collective-permute-start.2 = (f16[256,512]{1,0:T(8,128)(2,1)S(1)}, f16[256,512]{1,0:T(8,128)(2,1)S(1)}, u32[]{:S(2)}, u32[]{:S(2)}) collective-permute-start(f16[256,512]{1,0:T(8,128)(2,1)S(1)} %fusion.24), channel_id=1, source_target_pairs={{0,16},{4,20},{8,24},{12,28},{16,0},{20,4},{24,8},{28,12},{1,17},{... | collective-permute-start | bytes 786440 | tf_op jit(solution)/shard_map/ppermute | solution.py:19
  215.9 27.8 %collective-permute-start.5 = (f16[256,512]{1,0:T(8,128)(2,1)S(1)}, f16[256,512]{1,0:T(8,128)(2,1)S(1)}, u32[]{:S(2)}, u32[]{:S(2)}) collective-permute-start(f16[256,512]{1,0:T(8,128)(2,1)S(1)} %fusion.25), channel_id=1, source_target_pairs={{0,4},{4,0},{8,12},{12,8},{16,20},{20,16},{24,28},{28,24},{1,5},{5... | collective-permute-start | bytes 786440 | tf_op jit(solution)/shard_map/ppermute | solution.py:19
  225.0 24.0 %collective-permute-start.8 = (f16[256,512]{1,0:T(8,128)(2,1)S(1)}, f16[256,512]{1,0:T(8,128)(2,1)S(1)}, u32[]{:S(2)}, u32[]{:S(2)}) collective-permute-start(f16[256,512]{1,0:T(8,128)(2,1)S(1)} %fusion.26), channel_id=1, source_target_pairs={{0,16},{4,20},{8,24},{12,28},{16,0},{20,4},{24,8},{28,12},{1,17},{... | collective-permute-start | bytes 786440 | tf_op jit(solution)/shard_map/ppermute | solution.py:19
  226.8 22.4 %collective-permute-start.11 = (f16[256,512]{1,0:T(8,128)(2,1)S(1)}, f16[256,512]{1,0:T(8,128)(2,1)S(1)}, u32[]{:S(2)}, u32[]{:S(2)}) collective-permute-start(f16[256,512]{1,0:T(8,128)(2,1)S(1)} %fusion.27), channel_id=1, source_target_pairs={{0,4},{4,0},{8,12},{12,8},{16,20},{20,16},{24,28},{28,24},{1,5},{5... | collective-permute-start | bytes 786440 | tf_op jit(solution)/shard_map/ppermute | solution.py:19
  249.2 6.4 %copy-start.10 = (f32[1,512]{1,0:T(1,128)S(1)}, f32[1,512]{1,0:T(1,128)}, u32[]{:S(2)}) copy-start(f32[1,512]{1,0:T(1,128)} %param.7) | copy-start | bytes 6148
  249.2 26.5 %copy-start.9 = (f32[1,1024]{1,0:T(1,128)S(1)}, f32[1,1024]{1,0:T(1,128)}, u32[]{:S(2)}) copy-start(f32[1,1024]{1,0:T(1,128)} %param.8) | copy-start | bytes 12292
  256.3 64.3 %copy-start.8 = (f32[1,512]{1,0:T(1,128)}, f32[1,512]{1,0:T(1,128)S(1)}, u32[]{:S(2)}) copy-start(f32[1,512]{1,0:T(1,128)S(1)} %get-tuple-element.44) | copy-start | bytes 6148
  275.8 44.9 %copy-start.7 = (f32[1,1024]{1,0:T(1,128)}, f32[1,1024]{1,0:T(1,128)S(1)}, u32[]{:S(2)}) copy-start(f32[1,1024]{1,0:T(1,128)S(1)} %multiply_add_fusion.1) | copy-start | bytes 12292
  (4 other events, 11.8 us)
Sparse Core Ops, SparseCore 0:
  18.6 60.9 all-gather.3
  81.8 58.2 all-gather.5
  320.8 126.4 all-gather.7

commit v2 on v1

--- a/solution.py
+++ b/solution.py
@@ -1,6 +1,10 @@
+import functools
+
 import jax
 import jax.numpy as jnp
 from jax import lax
+from jax.experimental import pallas as pl
+from jax.experimental.pallas import tpu as pltpu
 from jax.sharding import PartitionSpec as P
 
 D = 4096
@@ -54,12 +58,240 @@
     return jnp.concatenate(pieces, axis=0)
 
 
+MESH = pl.DeviceIdType.MESH
+CHUNK = 64
+
+
+def exchange(axis, n, source, slots, send, recv):
+    me = lax.axis_index(axis)
+
+    def copy(to, slot):
+        return pltpu.make_async_remote_copy(
+            src_ref=source,
+            dst_ref=slots.at[slot],
+            send_sem=send.at[to],
+            recv_sem=recv.at[slot],
+            device_id={axis: to},
+            device_id_type=MESH,
+        )
+
+    def start():
+        for k in range(1, n):
+            copy(lax.rem(me + k, n), me).start()
+        slots[me] = source[...]
+
+    def finish():
+        for k in range(1, n):
+            peer = lax.rem(me + k, n)
+            copy(peer, peer).wait_recv()
+        for k in range(1, n):
+            copy(lax.rem(me + k, n), me).wait_send()
+
+    return start, finish
+
+
+def tail_kernel(
+    rows_n, cols_n, grad, row_part, col_part, row_stat, col_stat, master,
+    fresh, master_out, update, row_out, col_out,
+    row_slots, col_slots, row_tall, pair, pair_slots, one, one_slots,
+    rs, rr, cs, cr, ps, pr, os, orr, item_send, item_recv,
+):
+    r, c = lax.axis_index("row"), lax.axis_index("col")
+    height, width = grad.shape
+    y, z = lax.rem(r, 2), r // 2
+    depth = rows_n // 2
+    barrier = pltpu.get_barrier_semaphore()
+    for k in range(1, rows_n):
+        pl.semaphore_signal(barrier, inc=1, device_id={"row": lax.rem(r + k, rows_n)}, device_id_type=MESH)
+    for k in range(1, cols_n):
+        pl.semaphore_signal(barrier, inc=1, device_id={"col": lax.rem(c + k, cols_n)}, device_id_type=MESH)
+    pl.semaphore_wait(barrier, rows_n + cols_n - 2)
+
+    start_c, finish_c = exchange("row", rows_n, col_part, col_slots, cs, cr)
+    start_r, finish_r = exchange("col", cols_n, row_part, row_slots, rs, rr)
+    start_c()
+    start_r()
+    finish_r()
+    new_row = 0.75 * row_stat[...] + 0.25 * jnp.sum(row_slots[...], axis=0) / D
+    row_out[...] = new_row[0:1]
+    row_tall[...] = jnp.transpose(jnp.broadcast_to(new_row[0:1], (128, height)))
+    pair[8:16] = jnp.broadcast_to(jnp.sum(new_row, axis=1, keepdims=True), (8, 128))
+    finish_c()
+    new_col = 0.75 * col_stat[...] + 0.25 * jnp.sum(col_slots[...], axis=0) / D
+    col_out[...] = new_col[0:1]
+
+    def scaled(i, total):
+        here = pl.ds(pl.multiple_of(i * CHUNK, CHUNK), CHUNK)
+        value = grad[here] * lax.rsqrt(row_tall[here][:, 0:1] * col_out[...])
+        update[here] = value
+        return total + jnp.sum((value * value).reshape(CHUNK // 8, 8, width), axis=0)
+
+    total = lax.fori_loop(0, height // CHUNK, scaled, jnp.zeros((8, width), jnp.float32))
+    total = jnp.sum(jnp.sum(total, axis=0, keepdims=True), axis=1, keepdims=True)
+    pair[0:8] = jnp.broadcast_to(total, (8, 128))
+    start_p, finish_p = exchange("row", rows_n, pair, pair_slots, ps, pr)
+    start_p()
+    finish_p()
+    both = jnp.sum(pair_slots[...], axis=0)
+    one[...] = both[0:8]
+    start_o, finish_o = exchange("col", cols_n, one, one_slots, os, orr)
+    start_o()
+    finish_o()
+    mean = both[8:16] / D
+    rms = jnp.sqrt(jnp.sum(one_slots[...], axis=0) * mean / (D * D))
+    factor = (jnp.sqrt(mean) / jnp.maximum(1.0, rms))[0:1, 0:1]
+
+    def finished(i, carry):
+        here = pl.ds(pl.multiple_of(i * CHUNK, CHUNK), CHUNK)
+        value = update[here] * factor
+        update[here] = value
+        value = master[here] - 0.01 * value
+        master_out[here] = value
+        fresh[pl.ds(pl.multiple_of(r * height + i * CHUNK, CHUNK), CHUNK)] = value.astype(jnp.bfloat16)
+        return carry
+
+    piece = height // 2
+
+    def item(zs, ys, half, way):
+        number = (zs * 2 + ys) * 2 + half
+        place = fresh.at[pl.ds(pl.multiple_of(number * piece, piece), piece)]
+        target = r + (1 - 2 * y) if way == 0 else (r + 2 if way == 1 else r - 2)
+        return pltpu.make_async_remote_copy(
+            src_ref=place,
+            dst_ref=place,
+            send_sem=item_send.at[number * 3 + way],
+            recv_sem=item_recv.at[number],
+            device_id={"row": target},
+            device_id_type=MESH,
+        )
+
+    def along(zs, ys, half, way, act):
+        @pl.when(z < depth - 1 if way == 1 else z > 0)
+        def _():
+            act(item(zs, ys, half, way))
+
+    def begin(copy):
+        copy.start()
+
+    def sent(copy):
+        copy.wait_send()
+
+    def arrived(copy):
+        copy.wait_recv()
+
+    lax.fori_loop(0, height // CHUNK // 2, finished, 0)
+    item(z, y, 0, 0).start()
+    for way in (1, 2):
+        along(z, y, 0, way, begin)
+    lax.fori_loop(height // CHUNK // 2, height // CHUNK, finished, 0)
+    for way in (1, 2):
+        along(z, y, 1, way, begin)
+    item(z, y, 1, 0).start()
+    item(z, 1 - y, 0, 0).wait_recv()
+    for way in (1, 2):
+        along(z, 1 - y, 0, way, begin)
+
+    kinds = ((y, 0), (y, 1), (1 - y, 0))
+
+    def each(k, way, do):
+        zs = z - k if way == 1 else z + k
+
+        @pl.when(zs >= 0 if way == 1 else zs < depth)
+        def _():
+            do(zs)
+
+    for k in range(1, depth):
+        for ys, half in kinds:
+            for way in (1, 2):
+                def pass_on(zs, ys=ys, half=half, way=way):
+                    arrived(item(zs, ys, half, 0))
+                    along(zs, ys, half, way, begin)
+                    if half == 1:
+                        item(zs, ys, half, 0).start()
+
+                each(k, way, pass_on)
+
+    for k in range(depth):
+        for way in (1, 2) if k else (1,):
+            def last(zs):
+                arrived(item(zs, 1 - y, 1, 0))
+                sent(item(zs, y, 1, 0))
+
+            each(k, way, last)
+    item(z, y, 0, 0).wait_send()
+    for k in range(depth):
+        for ys, half in kinds:
+            for way in (1, 2):
+                def drain(zs, ys=ys, half=half, way=way):
+                    along(zs, ys, half, way, sent)
+
+                each(k, way, drain)
+
+
+def tail(grad, row_part, col_part, row_stat, col_stat, master):
+    rows_n, cols_n = lax.axis_size("row"), lax.axis_size("col")
+    height, width = grad.shape
+    f32 = jnp.float32
+
+    def eight(x):
+        return jnp.broadcast_to(x, (8, x.shape[1]))
+
+    vmem = pl.BlockSpec(memory_space=pltpu.VMEM)
+    dma = pltpu.SemaphoreType.DMA
+    items = rows_n * 2
+    return pl.pallas_call(
+        functools.partial(tail_kernel, rows_n, cols_n),
+        out_shape=(
+            jax.ShapeDtypeStruct((rows_n * height, width), jnp.bfloat16),
+            jax.ShapeDtypeStruct((height, width), f32),
+            jax.ShapeDtypeStruct((height, width), f32),
+            jax.ShapeDtypeStruct((1, height), f32),
+            jax.ShapeDtypeStruct((1, width), f32),
+        ),
+        in_specs=[vmem] * 6,
+        out_specs=(vmem,) * 5,
+        scratch_shapes=[
+            pltpu.VMEM((cols_n, 8, height), f32),
+            pltpu.VMEM((rows_n, 8, width), f32),
+            pltpu.VMEM((height, 128), f32),
+            pltpu.VMEM((16, 128), f32),
+            pltpu.VMEM((rows_n, 16, 128), f32),
+            pltpu.VMEM((8, 128), f32),
+            pltpu.VMEM((cols_n, 8, 128), f32),
+            dma((cols_n,)), dma((cols_n,)),
+            dma((rows_n,)), dma((rows_n,)),
+            dma((rows_n,)), dma((rows_n,)),
+            dma((cols_n,)), dma((cols_n,)),
+            dma((items * 3,)), dma((items,)),
+        ],
+        compiler_params=pltpu.CompilerParams(
+            collective_id=0, has_side_effects=True, vmem_limit_bytes=40 * 1024 * 1024
+        ),
+    )(grad, eight(row_part), eight(col_part), eight(row_stat), eight(col_stat), master)
+
+
 def shards(acts, out_grads, row_stat, col_stat, master):
     tok_here, mats, width_c = out_grads.shape
     flat_out = out_grads.reshape(tok_here, mats * width_c)
     rows_here = master.shape[0]
-    if (lax.axis_size("row"), lax.axis_size("col")) == (8, 4):
+    if (lax.axis_size("row"), lax.axis_size("col"), mats) == (8, 4, 1):
         grad = gradient_rows(acts, flat_out)
+        squares = grad * grad + 1e-30
+        fresh, master_out, update_out, row_out, col_out = tail(
+            grad,
+            jnp.sum(squares, axis=1)[None],
+            jnp.sum(squares, axis=0)[None],
+            row_stat,
+            col_stat,
+            master.reshape(rows_here, width_c),
+        )
+        return (
+            fresh.reshape(-1, mats, width_c),
+            master_out.reshape(master.shape),
+            update_out.reshape(master.shape),
+            row_out,
+            col_out,
+        )
     else:
         acts_full = lax.all_gather(acts, "col", axis=1, tiled=True)
         grad = lax.psum_scatter(

time: 462 us -> 399 us (0.86)
  Pallas kernels: 0 us -> 125 us
  waiting for transfers between devices: 259 us -> 137 us
  blocking collectives: 86.4 us -> 23.7 us
    pallas_call x0 -> x1, Pallas kernels: none -> 125 us  [tail(): pl.pallas_call(functools.partial(tail_kernel, rows_n, cols_n), out_shape=...]
    all_gather x1 -> x0, waiting for transfers between devices: 118 us -> none  [shards(): lax.all_gather(master_out.astype(jnp.bfloat16), 'row', axis=0, tiled=True)]
    psum x3 -> x0, blocking collectives: 62.7 us -> none  [the longest x1 37.3 us: shards(): total_sq = lax.psum(jnp.sum(raw * raw, axis=(0, 2)), ('row', 'col'))]
    convert_element_type x1 -> x0, other arithmetic: 4.72 us -> none  [shards(): master_out.astype(jnp.bfloat16)]
    unnamed x30 -> x27, local copies, waits for them, and re-layouts: 26.7 us -> 27.5 us
  transfers between devices with their start and end apart: 15 -> 14, of which waited for: 9 -> 8; matrix products, arithmetic and copies ran while one was open for 9% -> 10% of each run, Pallas kernels for 0% -> 0%
where the time goes in v2:
time: 399 us; the launch traced here: 398 us
  waiting for transfers between devices  137 us (34%)
  Pallas kernels  125 us (31%)
  local copies, waits for them, and re-layouts  32.4 us (8%)
  starting transfers between devices  27.2 us (7%)
  matrix products  24.6 us (6%)
  blocking collectives  23.7 us (6%)
  between operations  15.1 us (4%)
  other arithmetic  12.5 us (3%)
    pallas_call x1, Pallas kernels, tail(): pl.pallas_call(functools.partial(tail_kernel, rows_n, cols_n), out_shape=...  125 us
    all_gather x2, waiting for transfers between devices, gradient_rows(): full = lax.all_gather(mine, 'col', axis=1, tiled=True)  70.5 us
    ppermute x12, waiting for transfers between devices, pair_sum(): lax.ppermute((give * scale).astype(jnp.float16), 'row', [(r, r ^ partner_...  66.1 us
    unnamed x27, local copies, waits for them, and re-layouts  27.5 us
    ppermute x12, starting transfers between devices, pair_sum(): lax.ppermute((give * scale).astype(jnp.float16), 'row', [(r, r ^ partner_...  27.1 us
    dot_general x4, matrix products, contract_tokens(): lax.dot_general(left, right, (((0,), (0,)), ((), ())), preferred_element_...  24.6 us
    pmax x1, blocking collectives, gradient_rows(): top = lax.pmax(jnp.max(jnp.abs(flat_out)).astype(jnp.float32), 'row')  23.7 us
  transfers between devices with their start and end apart: 14, of which 8 were waited for; matrix products, arithmetic and copies ran while one was open for 10% of the time, Pallas kernels for 0%

profile of v2, /device:TPU:0, one launch (start us, length us, event | category | flops | bytes accessed | tf_op | source)
XLA Modules:
  0.0 398.1 jit_solution(1215368008005529949)
XLA Ops:
  7.2 6.4 %copy.22 = bf16[2048,1024]{0,1:T(8,128)(2,1)} copy(bf16[2048,1024]{1,0:T(8,128)(2,1)} %param.5) | data formatting | bytes 8388608 | tf_op args[0]
  13.6 4.8 %fusion.28 = (bf16[2048,2,1,256]{0,3,2,1:T(8,128)(2,1)}, bf16[2048,2,1,256]{0,3,2,1:T(8,128)(2,1)}) fusion(bf16[2048,2,2,256]{0,3,2,1:T(8,128)(2,1)} %bitcast.108), kind=kLoop, calls=%fused_computation.56 | loop fusion | bytes 8388608 | tf_op jit(solution)/shard_map/slice | solution.py:49
  19.2 3.8 abs_reduce_fusion
  23.0 23.7 %pmax.7 = f32[]{:T(128)} all-reduce(bf16[]{:T(256)} %abs_reduce_fusion), channel_id=1, replica_groups=mesh['row'=8,'col'=4] {'row'}, use_global_device_ids=true, to_apply=%region_1.0 | all-reduce | flops 1 | bytes 6 | tf_op jit(solution)/shard_map/pmax | solution.py:44
  46.8 2.1 copy.37
  49.5 30.1 %all-gather.3.cloned.1.call-done = bf16[2048,2048]{0,1:T(8,128)(2,1)} async-done(((bf16[2048,512]{0,1:T(8,128)(2,1)}), bf16[2048,2048]{0,1:T(8,128)(2,1)}) %all-gather.3.cloned.1.call-update) | async-done | bytes 8388624 | tf_op jit(solution)/shard_map/all_gather | solution.py:50
  79.6 7.7 %fusion.12 = f32[2048,512]{1,0:T(8,128)S(1)} fusion(bf16[2048,2048]{0,1:T(8,128)(2,1)} %all-gather.3.cloned.1.call-done, bf16[2048,1024]{1,0:T(8,128)(2,1)} %bitcast.112), kind=kOutput, calls=%fused_computation.24 | convolution fusion | flops 4294967296 | bytes 14680064 | tf_op jit(solution)/shard_map/dot_general | solution.py:14
  91.3 4.5 %fusion.8 = f32[2048,512]{1,0:T(8,128)S(1)} fusion(bf16[2048,2048]{0,1:T(8,128)(2,1)S(1)} %copy-done.9, bf16[2048,1024]{1,0:T(8,128)(2,1)S(1)} %bitcast.114), kind=kOutput, calls=%fused_computation.20 | convolution fusion | flops 4294967296 | bytes 14680064 | tf_op jit(solution)/shard_map/dot_general | solution.py:14
  95.8 2.0 copy-done.2
  99.7 40.4 %all-gather.5.cloned.1.call-done = bf16[2048,2048]{0,1:T(8,128)(2,1)} async-done(((bf16[2048,512]{0,1:T(8,128)(2,1)}), bf16[2048,2048]{0,1:T(8,128)(2,1)}) %all-gather.5.cloned.1.call-update) | async-done | bytes 8388624 | tf_op jit(solution)/shard_map/all_gather | solution.py:50
  140.1 7.8 %fusion.10 = f32[2048,512]{1,0:T(8,128)S(1)} fusion(bf16[2048,2048]{0,1:T(8,128)(2,1)} %all-gather.5.cloned.1.call-done, bf16[2048,1024]{1,0:T(8,128)(2,1)} %bitcast.113), kind=kOutput, calls=%fused_computation.22 | convolution fusion | flops 4294967296 | bytes 14680064 | tf_op jit(solution)/shard_map/dot_general | solution.py:14
  149.8 4.5 %fusion.6 = f32[2048,512]{1,0:T(8,128)S(1)} fusion(bf16[2048,2048]{0,1:T(8,128)(2,1)S(1)} %copy-done.8, bf16[2048,1024]{1,0:T(8,128)(2,1)S(1)} %bitcast.115), kind=kOutput, calls=%fused_computation.18 | convolution fusion | flops 4294967296 | bytes 14680064 | tf_op jit(solution)/shard_map/dot_general | solution.py:14
  160.4 2.5 collective-permute-start.4
  162.9 10.7 %collective-permute-done.6 = f16[2,2,256,512]{3,2,1,0:T(8,128)(2,1)S(1)} collective-permute-done((f16[2,2,256,512]{3,2,1,0:T(8,128)(2,1)S(1)}, f16[2,2,256,512]{3,2,1,0:T(8,128)(2,1)S(1)}, u32[]{:S(2)}, u32[]{:S(2)}) %collective-permute-start.6) | collective-permute-done | bytes 1048608 | tf_op jit(solution)/shard_map/ppermute | solution.py:23
  175.7 16.3 %collective-permute-done.9 = f16[2,2,256,512]{3,2,1,0:T(8,128)(2,1)S(1)} collective-permute-done((f16[2,2,256,512]{3,2,1,0:T(8,128)(2,1)S(1)}, f16[2,2,256,512]{3,2,1,0:T(8,128)(2,1)S(1)}, u32[]{:S(2)}, u32[]{:S(2)}) %collective-permute-start.9) | collective-permute-done | bytes 1048608 | tf_op jit(solution)/shard_map/ppermute | solution.py:23
  194.0 9.4 %collective-permute-done.1 = f16[2,256,512]{2,1,0:T(8,128)(2,1)S(1)} collective-permute-done((f16[2,256,512]{2,1,0:T(8,128)(2,1)S(1)}, f16[2,256,512]{2,1,0:T(8,128)(2,1)S(1)}, u32[]{:S(2)}, u32[]{:S(2)}) %collective-permute-start.1) | collective-permute-done | bytes 524320 | tf_op jit(solution)/shard_map/ppermute | solution.py:23
  203.5 12.1 %collective-permute-start.2 = (f16[256,512]{1,0:T(8,128)(2,1)S(1)}, f16[256,512]{1,0:T(8,128)(2,1)S(1)}, u32[]{:S(2)}, u32[]{:S(2)}) collective-permute-start(f16[256,512]{1,0:T(8,128)(2,1)S(1)} %fusion.24), channel_id=1, source_target_pairs={{0,16},{4,20},{8,24},{12,28},{16,0},{20,4},{24,8},{28,12},{1,17},{... | collective-permute-start | bytes 786440 | tf_op jit(solution)/shard_map/ppermute | solution.py:23
  216.5 8.2 %collective-permute-done.7 = f16[2,256,512]{2,1,0:T(8,128)(2,1)S(1)} collective-permute-done((f16[2,256,512]{2,1,0:T(8,128)(2,1)S(1)}, f16[2,256,512]{2,1,0:T(8,128)(2,1)S(1)}, u32[]{:S(2)}, u32[]{:S(2)}) %collective-permute-start.7) | collective-permute-done | bytes 524320 | tf_op jit(solution)/shard_map/ppermute | solution.py:23
  227.4 16.2 %collective-permute-done.2 = f16[256,512]{1,0:T(8,128)(2,1)S(1)} collective-permute-done((f16[256,512]{1,0:T(8,128)(2,1)S(1)}, f16[256,512]{1,0:T(8,128)(2,1)S(1)}, u32[]{:S(2)}, u32[]{:S(2)}) %collective-permute-start.2) | collective-permute-done | bytes 262176 | tf_op jit(solution)/shard_map/ppermute | solution.py:23
  243.8 5.3 %collective-permute-done.8 = f16[256,512]{1,0:T(8,128)(2,1)S(1)} collective-permute-done((f16[256,512]{1,0:T(8,128)(2,1)S(1)}, f16[256,512]{1,0:T(8,128)(2,1)S(1)}, u32[]{:S(2)}, u32[]{:S(2)}) %collective-permute-start.8) | collective-permute-done | bytes 262176 | tf_op jit(solution)/shard_map/ppermute | solution.py:23
  249.9 125.4 %shard_map.92 = (bf16[4096,1024]{1,0:T(8,128)(2,1)}, f32[512,1024]{1,0:T(8,128)S(1)}, f32[512,1024]{1,0:T(8,128)S(1)}, f32[1,512]{1,0:T(1,128)S(1)}, f32[1,1024]{1,0:T(1,128)S(1)}) custom-call(f32[512,1024]{1,0:T(8,128)S(1)} %get-tuple-element.34.grad, f32[8,512]{1,0:T(8,128)S(1)} %broadcast_in_dim.12.row_part, f32[8,1024]{1,0:T(8,128)S(1)} %broadcast_in_dim.13.col_part, ...), custom_call_target="tpu_custom_call" | custom-call | tf_op jit(solution)/shard_map/pallas_call | solution.py:242
  375.4 3.5 copy.29
  378.9 3.5 copy.30
  382.3 7.8 %copy.41 = bf16[4096,1,1024]{2,0,1:T(8,128)(2,1)} copy(bf16[4096,1,1024]{2,0,1:T(8,128)(2,1)} %bitcast.109) | data formatting | bytes 16777216
  (70 shorter events, 24.4 us)
Async XLA Ops:
  7.2 72.5 %all-gather.3.cloned.1.call-start = ((), (), s32[]{:S(2)}) async-start(), calls=%async_computation | async-start | bytes 10485760 | tf_op jit(solution)/shard_map/all_gather | solution.py:50
  18.5 121.6 %all-gather.5.cloned.1.call-start = ((), (), s32[]{:S(2)}) async-start(), calls=%async_computation.1 | async-start | bytes 10485760 | tf_op jit(solution)/shard_map/all_gather | solution.py:50
  79.6 11.6 %copy-start = (bf16[2048,1,1024]{2,0,1:T(8,128)(2,1)S(1)}, bf16[2048,1,1024]{2,0,1:T(8,128)(2,1)}, u32[]{:S(2)}) copy-start(bf16[2048,1,1024]{2,0,1:T(8,128)(2,1)} %param.6) | copy-start | bytes 12582916
  79.6 11.6 %copy-start.9 = (bf16[2048,2048]{0,1:T(8,128)(2,1)S(1)}, bf16[2048,2048]{0,1:T(8,128)(2,1)}, u32[]{:S(2)}) copy-start(bf16[2048,2048]{0,1:T(8,128)(2,1)} %all-gather.3.cloned.1.call-done) | copy-start | bytes 25165828
  87.3 2.5 copy-start.4
  89.8 66.4 %collective-permute-start = (f16[2,2,256,512]{3,2,1,0:T(8,128)(2,1)}, f16[2,2,256,512]{3,2,1,0:T(8,128)(2,1)}, u32[]{:S(2)}, u32[]{:S(2)}) collective-permute-start(f16[2,2,256,512]{3,2,1,0:T(8,128)(2,1)} %fusion.14), channel_id=1, source_target_pairs={{0,4},{4,0},{8,12},{12,8},{16,20},{20,16},{24,28},{28,24},{1,5},{5... | collective-permute-start | bytes 3145736 | tf_op jit(solution)/shard_map/ppermute | solution.py:23
  95.8 2.0 copy-start.2
  98.1 60.6 %collective-permute-start.3 = (f16[2,2,256,512]{3,2,1,0:T(8,128)(2,1)S(1)}, f16[2,2,256,512]{3,2,1,0:T(8,128)(2,1)}, u32[]{:S(2)}, u32[]{:S(2)}) collective-permute-start(f16[2,2,256,512]{3,2,1,0:T(8,128)(2,1)S(1)} %fusion.15), channel_id=1, source_target_pairs={{0,8},{4,12},{8,0},{12,4},{16,24},{20,28},{24,16},{28,20},{1,9},{5... | collective-permute-start | bytes 3145736 | tf_op jit(solution)/shard_map/ppermute | solution.py:23
  140.1 9.7 %copy-start.1 = (bf16[2048,1,1024]{2,0,1:T(8,128)(2,1)S(1)}, bf16[2048,1,1024]{2,0,1:T(8,128)(2,1)}, u32[]{:S(2)}) copy-start(bf16[2048,1,1024]{2,0,1:T(8,128)(2,1)} %param.6) | copy-start | bytes 12582916
  140.1 9.7 %copy-start.8 = (bf16[2048,2048]{0,1:T(8,128)(2,1)S(1)}, bf16[2048,2048]{0,1:T(8,128)(2,1)}, u32[]{:S(2)}) copy-start(bf16[2048,2048]{0,1:T(8,128)(2,1)} %all-gather.5.cloned.1.call-done) | copy-start | bytes 25165828
  148.2 25.4 %collective-permute-start.6 = (f16[2,2,256,512]{3,2,1,0:T(8,128)(2,1)S(1)}, f16[2,2,256,512]{3,2,1,0:T(8,128)(2,1)S(1)}, u32[]{:S(2)}, u32[]{:S(2)}) collective-permute-start(f16[2,2,256,512]{3,2,1,0:T(8,128)(2,1)S(1)} %fusion.16), channel_id=1, source_target_pairs={{0,4},{4,0},{8,12},{12,8},{16,20},{20,16},{24,28},{28,24},{1,5},{5... | collective-permute-start | bytes 3145736 | tf_op jit(solution)/shard_map/ppermute | solution.py:23
  149.8 6.4 %copy-start.5 = (f32[2048,512]{1,0:T(8,128)S(1)}, f32[2048,512]{1,0:T(8,128)}, u32[]{:S(2)}) copy-start(f32[2048,512]{1,0:T(8,128)} %copy-done.4) | copy-start | bytes 12582916
  154.6 37.3 %collective-permute-start.9 = (f16[2,2,256,512]{3,2,1,0:T(8,128)(2,1)S(1)}, f16[2,2,256,512]{3,2,1,0:T(8,128)(2,1)S(1)}, u32[]{:S(2)}, u32[]{:S(2)}) collective-permute-start(f16[2,2,256,512]{3,2,1,0:T(8,128)(2,1)S(1)} %fusion.17), channel_id=1, source_target_pairs={{0,8},{4,12},{8,0},{12,4},{16,24},{20,28},{24,16},{28,20},{1,9},{5... | collective-permute-start | bytes 3145736 | tf_op jit(solution)/shard_map/ppermute | solution.py:23
  156.2 2.5 copy-start.3
  158.0 45.3 %collective-permute-start.1 = (f16[2,256,512]{2,1,0:T(8,128)(2,1)S(1)}, f16[2,256,512]{2,1,0:T(8,128)(2,1)S(1)}, u32[]{:S(2)}, u32[]{:S(2)}) collective-permute-start(f16[2,256,512]{2,1,0:T(8,128)(2,1)S(1)} %fusion.22), channel_id=1, source_target_pairs={{0,8},{4,12},{8,0},{12,4},{16,24},{20,28},{24,16},{28,20},{1,9},{5... | collective-permute-start | bytes 1572872 | tf_op jit(solution)/shard_map/ppermute | solution.py:23
  160.4 55.2 %collective-permute-start.4 = (f16[2,256,512]{2,1,0:T(8,128)(2,1)S(1)}, f16[2,256,512]{2,1,0:T(8,128)(2,1)S(1)}, u32[]{:S(2)}, u32[]{:S(2)}) collective-permute-start(f16[2,256,512]{2,1,0:T(8,128)(2,1)S(1)} %fusion.20), channel_id=1, source_target_pairs={{0,16},{4,20},{8,24},{12,28},{16,0},{20,4},{24,8},{28,12},{1,17},{... | collective-permute-start | bytes 1572872 | tf_op jit(solution)/shard_map/ppermute | solution.py:23
  174.1 50.6 %collective-permute-start.7 = (f16[2,256,512]{2,1,0:T(8,128)(2,1)S(1)}, f16[2,256,512]{2,1,0:T(8,128)(2,1)S(1)}, u32[]{:S(2)}, u32[]{:S(2)}) collective-permute-start(f16[2,256,512]{2,1,0:T(8,128)(2,1)S(1)} %fusion.23), channel_id=1, source_target_pairs={{0,8},{4,12},{8,0},{12,4},{16,24},{20,28},{24,16},{28,20},{1,9},{5... | collective-permute-start | bytes 1572872 | tf_op jit(solution)/shard_map/ppermute | solution.py:23
  192.5 34.0 %collective-permute-start.10 = (f16[2,256,512]{2,1,0:T(8,128)(2,1)S(1)}, f16[2,256,512]{2,1,0:T(8,128)(2,1)S(1)}, u32[]{:S(2)}, u32[]{:S(2)}) collective-permute-start(f16[2,256,512]{2,1,0:T(8,128)(2,1)S(1)} %fusion.21), channel_id=1, source_target_pairs={{0,16},{4,20},{8,24},{12,28},{16,0},{20,4},{24,8},{28,12},{1,17},{... | collective-permute-start | bytes 1572872 | tf_op jit(solution)/shard_map/ppermute | solution.py:23
  203.5 40.0 %collective-permute-start.2 = (f16[256,512]{1,0:T(8,128)(2,1)S(1)}, f16[256,512]{1,0:T(8,128)(2,1)S(1)}, u32[]{:S(2)}, u32[]{:S(2)}) collective-permute-start(f16[256,512]{1,0:T(8,128)(2,1)S(1)} %fusion.24), channel_id=1, source_target_pairs={{0,16},{4,20},{8,24},{12,28},{16,0},{20,4},{24,8},{28,12},{1,17},{... | collective-permute-start | bytes 786440 | tf_op jit(solution)/shard_map/ppermute | solution.py:23
  215.9 27.8 %collective-permute-start.5 = (f16[256,512]{1,0:T(8,128)(2,1)S(1)}, f16[256,512]{1,0:T(8,128)(2,1)S(1)}, u32[]{:S(2)}, u32[]{:S(2)}) collective-permute-start(f16[256,512]{1,0:T(8,128)(2,1)S(1)} %fusion.25), channel_id=1, source_target_pairs={{0,4},{4,0},{8,12},{12,8},{16,20},{20,16},{24,28},{28,24},{1,5},{5... | collective-permute-start | bytes 786440 | tf_op jit(solution)/shard_map/ppermute | solution.py:23
  225.0 24.0 %collective-permute-start.8 = (f16[256,512]{1,0:T(8,128)(2,1)S(1)}, f16[256,512]{1,0:T(8,128)(2,1)S(1)}, u32[]{:S(2)}, u32[]{:S(2)}) collective-permute-start(f16[256,512]{1,0:T(8,128)(2,1)S(1)} %fusion.26), channel_id=1, source_target_pairs={{0,16},{4,20},{8,24},{12,28},{16,0},{20,4},{24,8},{28,12},{1,17},{... | collective-permute-start | bytes 786440 | tf_op jit(solution)/shard_map/ppermute | solution.py:23
  226.8 22.4 %collective-permute-start.11 = (f16[256,512]{1,0:T(8,128)(2,1)S(1)}, f16[256,512]{1,0:T(8,128)(2,1)S(1)}, u32[]{:S(2)}, u32[]{:S(2)}) collective-permute-start(f16[256,512]{1,0:T(8,128)(2,1)S(1)} %fusion.27), channel_id=1, source_target_pairs={{0,4},{4,0},{8,12},{12,8},{16,20},{20,16},{24,28},{28,24},{1,5},{5... | collective-permute-start | bytes 786440 | tf_op jit(solution)/shard_map/ppermute | solution.py:23
  249.2 0.7 copy-start.6
  249.2 0.7 copy-start.7
Sparse Core Ops, SparseCore 0:
  18.6 60.9 all-gather.2
  81.8 58.2 all-gather.4

commit v3 on v2

--- a/solution.py
+++ b/solution.py
@@ -26,15 +26,19 @@
     return keep + got.astype(jnp.float32) / scale
 
 
-def reduce_blocks(part, r, y_first, scale):
+def two_swaps(part, r, y_first, scale):
     y, z_lo, z_hi = r % 2, (r // 2) % 2, r // 4
     if y_first:
         part = pair_sum(part, 2, 1, y, scale)
-        part = pair_sum(part, 1, 2, z_lo, scale)
-        return pair_sum(part, 0, 4, z_hi, scale)
+        return pair_sum(part, 1, 2, z_lo, scale)
     part = pair_sum(part, 1, 2, z_lo, scale)
-    part = pair_sum(part, 0, 4, z_hi, scale)
-    return pair_sum(part, 0, 1, y, scale)
+    return pair_sum(part, 0, 4, z_hi, scale)
+
+
+def last_swap(part, r, y_first, scale):
+    if y_first:
+        return pair_sum(part, 0, 4, r // 4, scale)
+    return pair_sum(part, 0, 1, r % 2, scale)
 
 
 def gradient_rows(acts, flat_out):
@@ -45,21 +49,25 @@
     scale = 16384.0 / (6.0 * tok * lax.axis_size("row") * jnp.maximum(top, 1e-30))
     step = width // 4
     pieces = []
+    sums = []
     for k in range(2):
         mine = acts.reshape(tok, 2, 2, step)[:, :, k].reshape(tok, 2 * step)
         full = lax.all_gather(mine, "col", axis=1, tiled=True)
         half = cols // 2
+        if k == 1:
+            full, *sums = lax.optimization_barrier((full, *sums))
+            pieces.append([last_swap(sums[j], r, j == 0, scale) for j in range(2)])
         sums = []
         for j in range(2):
             part = contract_tokens(full, flat_out[:, j * half : (j + 1) * half])
             part = part.reshape(2, 2, 2, step, half)
-            sums.append(reduce_blocks(part, r, j == 0, scale))
-        pieces.append(jnp.concatenate(sums, axis=1))
-    return jnp.concatenate(pieces, axis=0)
+            sums.append(two_swaps(part, r, j == 0, scale))
+    pieces.append([last_swap(sums[j], r, j == 0, scale) for j in range(2)])
+    return jnp.concatenate([jnp.concatenate(p, axis=1) for p in pieces], axis=0)
 
 
 MESH = pl.DeviceIdType.MESH
-CHUNK = 64
+CHUNK = 32
 
 
 def exchange(axis, n, source, slots, send, recv):
@@ -150,11 +158,13 @@
         fresh[pl.ds(pl.multiple_of(r * height + i * CHUNK, CHUNK), CHUNK)] = value.astype(jnp.bfloat16)
         return carry
 
-    piece = height // 2
+    first = height * 3 // 16
+    cuts = (0, first, (height + first) // 2, height)
 
     def item(zs, ys, half, way):
-        number = (zs * 2 + ys) * 2 + half
-        place = fresh.at[pl.ds(pl.multiple_of(number * piece, piece), piece)]
+        number = (zs * 2 + ys) * 3 + half
+        begins = pl.multiple_of((zs * 2 + ys) * height + cuts[half], 16)
+        place = fresh.at[pl.ds(begins, cuts[half + 1] - cuts[half])]
         target = r + (1 - 2 * y) if way == 0 else (r + 2 if way == 1 else r - 2)
         return pltpu.make_async_remote_copy(
             src_ref=place,
@@ -179,19 +189,20 @@
     def arrived(copy):
         copy.wait_recv()
 
-    lax.fori_loop(0, height // CHUNK // 2, finished, 0)
+    lax.fori_loop(0, cuts[1] // CHUNK, finished, 0)
     item(z, y, 0, 0).start()
     for way in (1, 2):
         along(z, y, 0, way, begin)
-    lax.fori_loop(height // CHUNK // 2, height // CHUNK, finished, 0)
-    for way in (1, 2):
-        along(z, y, 1, way, begin)
-    item(z, y, 1, 0).start()
+    lax.fori_loop(cuts[1] // CHUNK, height // CHUNK, finished, 0)
+    for half in (1, 2):
+        for way in (1, 2):
+            along(z, y, half, way, begin)
+        item(z, y, half, 0).start()
     item(z, 1 - y, 0, 0).wait_recv()
     for way in (1, 2):
         along(z, 1 - y, 0, way, begin)
 
-    kinds = ((y, 0), (y, 1), (1 - y, 0))
+    kinds = ((y, 0), (y, 1), (y, 2), (1 - y, 0))
 
     def each(k, way, do):
         zs = z - k if way == 1 else z + k
@@ -206,7 +217,7 @@
                 def pass_on(zs, ys=ys, half=half, way=way):
                     arrived(item(zs, ys, half, 0))
                     along(zs, ys, half, way, begin)
-                    if half == 1:
+                    if half >= 1:
                         item(zs, ys, half, 0).start()
 
                 each(k, way, pass_on)
@@ -214,8 +225,9 @@
     for k in range(depth):
         for way in (1, 2) if k else (1,):
             def last(zs):
-                arrived(item(zs, 1 - y, 1, 0))
-                sent(item(zs, y, 1, 0))
+                for half in (1, 2):
+                    arrived(item(zs, 1 - y, half, 0))
+                    sent(item(zs, y, half, 0))
 
             each(k, way, last)
     item(z, y, 0, 0).wait_send()
@@ -238,7 +250,7 @@
 
     vmem = pl.BlockSpec(memory_space=pltpu.VMEM)
     dma = pltpu.SemaphoreType.DMA
-    items = rows_n * 2
+    items = rows_n * 3
     return pl.pallas_call(
         functools.partial(tail_kernel, rows_n, cols_n),
         out_shape=(

time: 399 us -> 371 us (0.930)
  Pallas kernels: 125 us -> 111 us
  waiting for transfers between devices: 137 us -> 128 us
  starting transfers between devices: 27.2 us -> 18.8 us
    all_gather x2, waiting for transfers between devices: 70.5 us -> 32.2 us  [gradient_rows(): full = lax.all_gather(mine, 'col', axis=1, tiled=True)]
    ppermute x12, waiting for transfers between devices: 66.1 us -> 95.5 us  [pair_sum(): lax.ppermute((give * scale).astype(jnp.float16), 'row', [(r, r ^ partner_...]
    pallas_call x1, Pallas kernels: 125 us -> 111 us  [tail(): pl.pallas_call(functools.partial(tail_kernel, rows_n, cols_n), out_shape=...]
    ppermute x12, starting transfers between devices: 27.1 us -> 18.7 us  [pair_sum(): lax.ppermute((give * scale).astype(jnp.float16), 'row', [(r, r ^ partner_...]
    unnamed x27 -> x31, local copies, waits for them, and re-layouts: 27.5 us -> 28.7 us
  transfers between devices with their start and end apart: 14 -> 14, of which waited for: 8 -> 11; matrix products, arithmetic and copies ran while one was open for 10% -> 9% of each run, Pallas kernels for 0% -> 0%
where the time goes in v3:
time: 371 us
  waiting for transfers between devices  128 us (35%)
  Pallas kernels  111 us (30%)
  local copies, waits for them, and re-layouts  33.6 us (9%)
  matrix products  24.6 us (7%)
  blocking collectives  23.7 us (6%)
  starting transfers between devices  18.8 us (5%)
  other arithmetic  15.7 us (4%)
  between operations  15.1 us (4%)
    pallas_call x1, Pallas kernels, tail(): pl.pallas_call(functools.partial(tail_kernel, rows_n, cols_n), out_shape=...  111 us
    ppermute x12, waiting for transfers between devices, pair_sum(): lax.ppermute((give * scale).astype(jnp.float16), 'row', [(r, r ^ partner_...  95.5 us
    all_gather x2, waiting for transfers between devices, gradient_rows(): full = lax.all_gather(mine, 'col', axis=1, tiled=True)  32.2 us
    unnamed x31, local copies, waits for them, and re-layouts  28.7 us
    dot_general x4, matrix products, contract_tokens(): lax.dot_general(left, right, (((0,), (0,)), ((), ())), preferred_element_...  24.6 us
    pmax x1, blocking collectives, gradient_rows(): top = lax.pmax(jnp.max(jnp.abs(flat_out)).astype(jnp.float32), 'row')  23.7 us
    ppermute x12, starting transfers between devices, pair_sum(): lax.ppermute((give * scale).astype(jnp.float16), 'row', [(r, r ^ partner_...  18.7 us
    add x12, other arithmetic, pair_sum(): return keep + got.astype(jnp.float32) / scale  7.94 us
  transfers between devices with their start and end apart: 14, of which 11 were waited for; matrix products, arithmetic and copies ran while one was open for 9% of the time, Pallas kernels for 0%

profile of v3, /device:TPU:0, one launch (start us, length us, event | category | flops | bytes accessed | tf_op | source)
XLA Modules:
  0.0 370.6 jit_solution(4133987756908914177)
XLA Ops:
  7.2 6.4 %copy.22 = bf16[2048,1024]{0,1:T(8,128)(2,1)} copy(bf16[2048,1024]{1,0:T(8,128)(2,1)} %param.5) | data formatting | bytes 8388608 | tf_op args[0]
  13.6 4.8 %fusion.28 = (bf16[2048,2,1,256]{0,3,2,1:T(8,128)(2,1)}, bf16[2048,2,1,256]{0,3,2,1:T(8,128)(2,1)}) fusion(bf16[2048,2,2,256]{0,3,2,1:T(8,128)(2,1)} %bitcast.108), kind=kLoop, calls=%fused_computation.56 | loop fusion | bytes 8388608 | tf_op jit(solution)/shard_map/slice | solution.py:54
  19.2 3.8 %abs_reduce_fusion = bf16[]{:T(256)} fusion(bf16[2048,1,1024]{2,0,1:T(8,128)(2,1)} %param.6), kind=kLoop, calls=%fused_computation | loop fusion | flops 4194303 | bytes 4194306 | tf_op jit(solution)/shard_map/reduce_max | solution.py:48
  23.0 23.7 %pmax.7 = f32[]{:T(128)} all-reduce(bf16[]{:T(256)} %abs_reduce_fusion), channel_id=1, replica_groups=mesh['row'=8,'col'=4] {'row'}, use_global_device_ids=true, to_apply=%region_1.0 | all-reduce | flops 1 | bytes 6 | tf_op jit(solution)/shard_map/pmax | solution.py:48
  47.4 32.2 %all-gather.5.cloned.1.call-done = bf16[2048,2048]{0,1:T(8,128)(2,1)} async-done(((bf16[2048,512]{0,1:T(8,128)(2,1)}), bf16[2048,2048]{0,1:T(8,128)(2,1)}) %all-gather.5.cloned.1.call-update) | async-done | bytes 8388624 | tf_op jit(solution)/shard_map/all_gather | solution.py:55
  79.6 7.7 %fusion.12 = f32[2048,512]{1,0:T(8,128)S(1)} fusion(bf16[2048,2048]{0,1:T(8,128)(2,1)} %all-gather.5.cloned.1.call-done, bf16[2048,1024]{1,0:T(8,128)(2,1)} %bitcast.112), kind=kOutput, calls=%fused_computation.24 | convolution fusion | flops 4294967296 | bytes 14680064 | tf_op jit(solution)/shard_map/dot_general | solution.py:14
  90.8 4.5 %fusion.8 = f32[2048,512]{1,0:T(8,128)S(1)} fusion(bf16[2048,2048]{0,1:T(8,128)(2,1)S(1)} %copy-done.11, bf16[2048,1024]{1,0:T(8,128)(2,1)S(1)} %bitcast.114), kind=kOutput, calls=%fused_computation.20 | convolution fusion | flops 4294967296 | bytes 14680064 | tf_op jit(solution)/shard_map/dot_general | solution.py:14
  99.2 15.6 %collective-permute-done = f16[2,2,256,512]{3,2,1,0:T(8,128)(2,1)} collective-permute-done((f16[2,2,256,512]{3,2,1,0:T(8,128)(2,1)S(1)}, f16[2,2,256,512]{3,2,1,0:T(8,128)(2,1)}, u32[]{:S(2)}, u32[]{:S(2)}) %collective-permute-start) | collective-permute-done | bytes 1048608 | tf_op jit(solution)/shard_map/ppermute | solution.py:23
  119.7 4.2 %collective-permute-done.2 = f16[2,2,256,512]{3,2,1,0:T(8,128)(2,1)} collective-permute-done((f16[2,2,256,512]{3,2,1,0:T(8,128)(2,1)S(1)}, f16[2,2,256,512]{3,2,1,0:T(8,128)(2,1)}, u32[]{:S(2)}, u32[]{:S(2)}) %collective-permute-start.2) | collective-permute-done | bytes 1048608 | tf_op jit(solution)/shard_map/ppermute | solution.py:23
  130.1 10.3 %collective-permute-done.1 = f16[2,256,512]{2,1,0:T(8,128)(2,1)} collective-permute-done((f16[2,256,512]{2,1,0:T(8,128)(2,1)}, f16[2,256,512]{2,1,0:T(8,128)(2,1)}, u32[]{:S(2)}, u32[]{:S(2)}) %collective-permute-start.1) | collective-permute-done | bytes 524320 | tf_op jit(solution)/shard_map/ppermute | solution.py:23
  141.6 10.6 %collective-permute-done.3 = f16[2,256,512]{2,1,0:T(8,128)(2,1)} collective-permute-done((f16[2,256,512]{2,1,0:T(8,128)(2,1)}, f16[2,256,512]{2,1,0:T(8,128)(2,1)}, u32[]{:S(2)}, u32[]{:S(2)}) %collective-permute-start.3) | collective-permute-done | bytes 524320 | tf_op jit(solution)/shard_map/ppermute | solution.py:23
  153.4 7.9 %fusion.10 = f32[2048,512]{1,0:T(8,128)S(1)} fusion(bf16[2048,2048]{0,1:T(8,128)(2,1)} %all-gather.3.cloned.1.call-done, bf16[2048,1024]{1,0:T(8,128)(2,1)} %bitcast.113), kind=kOutput, calls=%fused_computation.22 | convolution fusion | flops 4294967296 | bytes 14680064 | tf_op jit(solution)/shard_map/dot_general | solution.py:14
  162.2 4.5 %fusion.6 = f32[2048,512]{1,0:T(8,128)S(1)} fusion(bf16[2048,2048]{0,1:T(8,128)(2,1)S(1)} %copy-done.10, bf16[2048,1024]{1,0:T(8,128)(2,1)S(1)} %bitcast.115), kind=kOutput, calls=%fused_computation.18 | convolution fusion | flops 4294967296 | bytes 14680064 | tf_op jit(solution)/shard_map/dot_general | solution.py:14
  168.9 2.7 collective-permute-start.4
  173.2 13.6 %collective-permute-done.6 = f16[2,2,256,512]{3,2,1,0:T(8,128)(2,1)S(1)} collective-permute-done((f16[2,2,256,512]{3,2,1,0:T(8,128)(2,1)S(1)}, f16[2,2,256,512]{3,2,1,0:T(8,128)(2,1)S(1)}, u32[]{:S(2)}, u32[]{:S(2)}) %collective-permute-start.6) | collective-permute-done | bytes 1048608 | tf_op jit(solution)/shard_map/ppermute | solution.py:23
  187.9 11.4 %collective-permute-done.9 = f16[2,2,256,512]{3,2,1,0:T(8,128)(2,1)S(1)} collective-permute-done((f16[2,2,256,512]{3,2,1,0:T(8,128)(2,1)S(1)}, f16[2,2,256,512]{3,2,1,0:T(8,128)(2,1)S(1)}, u32[]{:S(2)}, u32[]{:S(2)}) %collective-permute-start.9) | collective-permute-done | bytes 1048608 | tf_op jit(solution)/shard_map/ppermute | solution.py:23
  199.8 4.0 %collective-permute-start.10 = (f16[2,256,512]{2,1,0:T(8,128)(2,1)S(1)}, f16[2,256,512]{2,1,0:T(8,128)(2,1)S(1)}, u32[]{:S(2)}, u32[]{:S(2)}) collective-permute-start(f16[2,256,512]{2,1,0:T(8,128)(2,1)S(1)} %fusion.21), channel_id=1, source_target_pairs={{0,16},{4,20},{8,24},{12,28},{16,0},{20,4},{24,8},{28,12},{1,17},{... | collective-permute-start | bytes 1572872 | tf_op jit(solution)/shard_map/ppermute | solution.py:23
  203.9 10.8 %collective-permute-done.7 = f16[2,256,512]{2,1,0:T(8,128)(2,1)S(1)} collective-permute-done((f16[2,256,512]{2,1,0:T(8,128)(2,1)S(1)}, f16[2,256,512]{2,1,0:T(8,128)(2,1)S(1)}, u32[]{:S(2)}, u32[]{:S(2)}) %collective-permute-start.7) | collective-permute-done | bytes 524320 | tf_op jit(solution)/shard_map/ppermute | solution.py:23
  215.1 14.5 %collective-permute-done.10 = f16[2,256,512]{2,1,0:T(8,128)(2,1)S(1)} collective-permute-done((f16[2,256,512]{2,1,0:T(8,128)(2,1)S(1)}, f16[2,256,512]{2,1,0:T(8,128)(2,1)S(1)}, u32[]{:S(2)}, u32[]{:S(2)}) %collective-permute-start.10) | collective-permute-done | bytes 524320 | tf_op jit(solution)/shard_map/ppermute | solution.py:23
  232.8 3.4 collective-permute-done.11
  237.1 110.8 %shard_map.92 = (bf16[4096,1024]{1,0:T(8,128)(2,1)}, f32[512,1024]{1,0:T(8,128)S(1)}, f32[512,1024]{1,0:T(8,128)S(1)}, f32[1,512]{1,0:T(1,128)S(1)}, f32[1,1024]{1,0:T(1,128)S(1)}) custom-call(f32[512,1024]{1,0:T(8,128)S(1)} %get-tuple-element.40.grad, f32[8,512]{1,0:T(8,128)S(1)} %broadcast_in_dim.12.row_part, f32[8,1024]{1,0:T(8,128)S(1)} %broadcast_in_dim.13.col_part, ...), custom_call_target="tpu_custom_call" | custom-call | tf_op jit(solution)/shard_map/pallas_call | solution.py:254
  347.9 3.5 copy.29
  351.4 3.5 copy.30
  354.8 7.8 %copy.41 = bf16[4096,1,1024]{2,0,1:T(8,128)(2,1)} copy(bf16[4096,1,1024]{2,0,1:T(8,128)(2,1)} %bitcast.109) | data formatting | bytes 16777216
  (74 shorter events, 33.5 us)
Async XLA Ops:
  7.2 72.5 %all-gather.5.cloned.1.call-start = ((), (), s32[]{:S(2)}) async-start(), calls=%async_computation.1 | async-start | bytes 10485760 | tf_op jit(solution)/shard_map/all_gather | solution.py:55
  18.5 134.9 %all-gather.3.cloned.1.call-start = ((), (), s32[]{:S(2)}) async-start(), calls=%async_computation | async-start | bytes 10485760 | tf_op jit(solution)/shard_map/all_gather | solution.py:55
  79.6 11.2 %copy-start.2 = (bf16[2048,1,1024]{2,0,1:T(8,128)(2,1)S(1)}, bf16[2048,1,1024]{2,0,1:T(8,128)(2,1)}, u32[]{:S(2)}) copy-start(bf16[2048,1,1024]{2,0,1:T(8,128)(2,1)} %param.6) | copy-start | bytes 12582916
  79.6 11.2 %copy-start.11 = (bf16[2048,2048]{0,1:T(8,128)(2,1)S(1)}, bf16[2048,2048]{0,1:T(8,128)(2,1)}, u32[]{:S(2)}) copy-start(bf16[2048,2048]{0,1:T(8,128)(2,1)} %all-gather.5.cloned.1.call-done) | copy-start | bytes 25165828
  87.3 2.0 copy-start.6
  89.3 25.4 %collective-permute-start = (f16[2,2,256,512]{3,2,1,0:T(8,128)(2,1)S(1)}, f16[2,2,256,512]{3,2,1,0:T(8,128)(2,1)}, u32[]{:S(2)}, u32[]{:S(2)}) collective-permute-start(f16[2,2,256,512]{3,2,1,0:T(8,128)(2,1)S(1)} %fusion.14), channel_id=1, source_target_pairs={{0,4},{4,0},{8,12},{12,8},{16,20},{20,16},{24,28},{28,24},{1,5},{5... | collective-permute-start | bytes 3145736 | tf_op jit(solution)/shard_map/ppermute | solution.py:23
  95.3 2.0 copy-start.4
  97.6 26.2 %collective-permute-start.2 = (f16[2,2,256,512]{3,2,1,0:T(8,128)(2,1)S(1)}, f16[2,2,256,512]{3,2,1,0:T(8,128)(2,1)}, u32[]{:S(2)}, u32[]{:S(2)}) collective-permute-start(f16[2,2,256,512]{3,2,1,0:T(8,128)(2,1)S(1)} %fusion.15), channel_id=1, source_target_pairs={{0,8},{4,12},{8,0},{12,4},{16,24},{20,28},{24,16},{28,20},{1,9},{5... | collective-permute-start | bytes 3145736 | tf_op jit(solution)/shard_map/ppermute | solution.py:23
  114.8 9.1 %copy-start.5 = (f32[2048,512]{1,0:T(8,128)S(1)}, f32[2048,512]{1,0:T(8,128)}, u32[]{:S(2)}) copy-start(f32[2048,512]{1,0:T(8,128)} %copy-done.4) | copy-start | bytes 12582916
  118.2 22.2 %collective-permute-start.1 = (f16[2,256,512]{2,1,0:T(8,128)(2,1)}, f16[2,256,512]{2,1,0:T(8,128)(2,1)}, u32[]{:S(2)}, u32[]{:S(2)}) collective-permute-start(f16[2,256,512]{2,1,0:T(8,128)(2,1)} %fusion.22), channel_id=1, source_target_pairs={{0,8},{4,12},{8,0},{12,4},{16,24},{20,28},{24,16},{28,20},{1,9},{5... | collective-permute-start | bytes 1572872 | tf_op jit(solution)/shard_map/ppermute | solution.py:23
  125.4 1.3 copy-start
  127.7 24.5 %collective-permute-start.3 = (f16[2,256,512]{2,1,0:T(8,128)(2,1)}, f16[2,256,512]{2,1,0:T(8,128)(2,1)}, u32[]{:S(2)}, u32[]{:S(2)}) collective-permute-start(f16[2,256,512]{2,1,0:T(8,128)(2,1)} %fusion.20), channel_id=1, source_target_pairs={{0,16},{4,20},{8,24},{12,28},{16,0},{20,4},{24,8},{28,12},{1,17},{... | collective-permute-start | bytes 1572872 | tf_op jit(solution)/shard_map/ppermute | solution.py:23
  130.1 22.1 %copy-start.1 = (f32[2,2,256,512]{3,2,1,0:T(8,128)S(1)}, f32[2,2,256,512]{3,2,1,0:T(8,128)}, u32[]{:S(2)}) copy-start(f32[2,2,256,512]{3,2,1,0:T(8,128)} %copy-done) | copy-start | bytes 6291460
  153.4 8.8 %copy-start.3 = (bf16[2048,1,1024]{2,0,1:T(8,128)(2,1)S(1)}, bf16[2048,1,1024]{2,0,1:T(8,128)(2,1)}, u32[]{:S(2)}) copy-start(bf16[2048,1,1024]{2,0,1:T(8,128)(2,1)} %param.6) | copy-start | bytes 12582916
  153.4 8.8 %copy-start.10 = (bf16[2048,2048]{0,1:T(8,128)(2,1)S(1)}, bf16[2048,2048]{0,1:T(8,128)(2,1)}, u32[]{:S(2)}) copy-start(bf16[2048,2048]{0,1:T(8,128)(2,1)} %all-gather.3.cloned.1.call-done) | copy-start | bytes 25165828
  161.6 25.2 %collective-permute-start.6 = (f16[2,2,256,512]{3,2,1,0:T(8,128)(2,1)S(1)}, f16[2,2,256,512]{3,2,1,0:T(8,128)(2,1)S(1)}, u32[]{:S(2)}, u32[]{:S(2)}) collective-permute-start(f16[2,2,256,512]{3,2,1,0:T(8,128)(2,1)S(1)} %fusion.16), channel_id=1, source_target_pairs={{0,4},{4,0},{8,12},{12,8},{16,20},{20,16},{24,28},{28,24},{1,5},{5... | collective-permute-start | bytes 3145736 | tf_op jit(solution)/shard_map/ppermute | solution.py:23
  166.8 1.6 copy-start.7
  167.1 32.2 %collective-permute-start.9 = (f16[2,2,256,512]{3,2,1,0:T(8,128)(2,1)S(1)}, f16[2,2,256,512]{3,2,1,0:T(8,128)(2,1)S(1)}, u32[]{:S(2)}, u32[]{:S(2)}) collective-permute-start(f16[2,2,256,512]{3,2,1,0:T(8,128)(2,1)S(1)} %fusion.17), channel_id=1, source_target_pairs={{0,8},{4,12},{8,0},{12,4},{16,24},{20,28},{24,16},{28,20},{1,9},{5... | collective-permute-start | bytes 3145736 | tf_op jit(solution)/shard_map/ppermute | solution.py:23
  168.9 34.9 %collective-permute-start.4 = (f16[256,512]{1,0:T(8,128)(2,1)S(1)}, f16[256,512]{1,0:T(8,128)(2,1)S(1)}, u32[]{:S(2)}, u32[]{:S(2)}) collective-permute-start(f16[256,512]{1,0:T(8,128)(2,1)S(1)} %fusion.24), channel_id=1, source_target_pairs={{0,16},{4,20},{8,24},{12,28},{16,0},{20,4},{24,8},{28,12},{1,17},{... | collective-permute-start | bytes 786440 | tf_op jit(solution)/shard_map/ppermute | solution.py:23
  171.7 59.7 %collective-permute-start.5 = (f16[256,512]{1,0:T(8,128)(2,1)S(1)}, f16[256,512]{1,0:T(8,128)(2,1)S(1)}, u32[]{:S(2)}, u32[]{:S(2)}) collective-permute-start(f16[256,512]{1,0:T(8,128)(2,1)S(1)} %fusion.25), channel_id=1, source_target_pairs={{0,4},{4,0},{8,12},{12,8},{16,20},{20,16},{24,28},{28,24},{1,5},{5... | collective-permute-start | bytes 786440 | tf_op jit(solution)/shard_map/ppermute | solution.py:23
  187.3 27.4 %collective-permute-start.7 = (f16[2,256,512]{2,1,0:T(8,128)(2,1)S(1)}, f16[2,256,512]{2,1,0:T(8,128)(2,1)S(1)}, u32[]{:S(2)}, u32[]{:S(2)}) collective-permute-start(f16[2,256,512]{2,1,0:T(8,128)(2,1)S(1)} %fusion.23), channel_id=1, source_target_pairs={{0,8},{4,12},{8,0},{12,4},{16,24},{20,28},{24,16},{28,20},{1,9},{5... | collective-permute-start | bytes 1572872 | tf_op jit(solution)/shard_map/ppermute | solution.py:23
  199.8 29.7 %collective-permute-start.10 = (f16[2,256,512]{2,1,0:T(8,128)(2,1)S(1)}, f16[2,256,512]{2,1,0:T(8,128)(2,1)S(1)}, u32[]{:S(2)}, u32[]{:S(2)}) collective-permute-start(f16[2,256,512]{2,1,0:T(8,128)(2,1)S(1)} %fusion.21), channel_id=1, source_target_pairs={{0,16},{4,20},{8,24},{12,28},{16,0},{20,4},{24,8},{28,12},{1,17},{... | collective-permute-start | bytes 1572872 | tf_op jit(solution)/shard_map/ppermute | solution.py:23
  215.0 17.7 %collective-permute-start.8 = (f16[256,512]{1,0:T(8,128)(2,1)S(1)}, f16[256,512]{1,0:T(8,128)(2,1)S(1)}, u32[]{:S(2)}, u32[]{:S(2)}) collective-permute-start(f16[256,512]{1,0:T(8,128)(2,1)S(1)} %fusion.26), channel_id=1, source_target_pairs={{0,16},{4,20},{8,24},{12,28},{16,0},{20,4},{24,8},{28,12},{1,17},{... | collective-permute-start | bytes 786440 | tf_op jit(solution)/shard_map/ppermute | solution.py:23
  229.8 6.4 %collective-permute-start.11 = (f16[256,512]{1,0:T(8,128)(2,1)S(1)}, f16[256,512]{1,0:T(8,128)(2,1)S(1)}, u32[]{:S(2)}, u32[]{:S(2)}) collective-permute-start(f16[256,512]{1,0:T(8,128)(2,1)S(1)} %fusion.27), channel_id=1, source_target_pairs={{0,4},{4,0},{8,12},{12,8},{16,20},{20,16},{24,28},{28,24},{1,5},{5... | collective-permute-start | bytes 786440 | tf_op jit(solution)/shard_map/ppermute | solution.py:23
  (2 other events, 1.4 us)
Sparse Core Ops, SparseCore 0:
  18.6 60.9 all-gather.4
  81.8 58.2 all-gather.2

commit v4 on v3

--- a/solution.py
+++ b/solution.py
@@ -55,7 +55,7 @@
         full = lax.all_gather(mine, "col", axis=1, tiled=True)
         half = cols // 2
         if k == 1:
-            full, *sums = lax.optimization_barrier((full, *sums))
+            full, sums[0] = lax.optimization_barrier((full, sums[0]))
             pieces.append([last_swap(sums[j], r, j == 0, scale) for j in range(2)])
         sums = []
         for j in range(2):

time: 371 us -> 367 us (0.989)
  waiting for transfers between devices: 128 us -> 119 us
  other arithmetic: 15.7 us -> 21.5 us
  starting transfers between devices: 18.8 us -> 14.2 us
    ppermute x12, waiting for transfers between devices: 95.5 us -> 86.6 us  [pair_sum(): lax.ppermute((give * scale).astype(jnp.float16), 'row', [(r, r ^ partner_...]
    ppermute x12, starting transfers between devices: 18.7 us -> 14.1 us  [pair_sum(): lax.ppermute((give * scale).astype(jnp.float16), 'row', [(r, r ^ partner_...]
    unnamed x31 -> x33, local copies, waits for them, and re-layouts: 28.7 us -> 32.3 us
  transfers between devices with their start and end apart: 14 -> 14, of which waited for: 11 -> 10; matrix products, arithmetic and copies ran while one was open for 9% -> 13% of each run, Pallas kernels for 0% -> 0%
where the time goes in v4:
time: 367 us; the launch traced here: 366 us
  waiting for transfers between devices  119 us (32%)
  Pallas kernels  111 us (30%)
  local copies, waits for them, and re-layouts  37.2 us (10%)
  matrix products  24.6 us (7%)
  blocking collectives  23.7 us (6%)
  other arithmetic  21.5 us (6%)
  between operations  15.1 us (4%)
  starting transfers between devices  14.2 us (4%)
    pallas_call x1, Pallas kernels, tail(): pl.pallas_call(functools.partial(tail_kernel, rows_n, cols_n), out_shape=...  111 us
    ppermute x12, waiting for transfers between devices, pair_sum(): lax.ppermute((give * scale).astype(jnp.float16), 'row', [(r, r ^ partner_...  86.6 us
    unnamed x33, local copies, waits for them, and re-layouts  32.3 us
    all_gather x2, waiting for transfers between devices, gradient_rows(): full = lax.all_gather(mine, 'col', axis=1, tiled=True)  32.2 us
    dot_general x4, matrix products, contract_tokens(): lax.dot_general(left, right, (((0,), (0,)), ((), ())), preferred_element_...  24.6 us
    pmax x1, blocking collectives, gradient_rows(): top = lax.pmax(jnp.max(jnp.abs(flat_out)).astype(jnp.float32), 'row')  23.7 us
    ppermute x12, starting transfers between devices, pair_sum(): lax.ppermute((give * scale).astype(jnp.float16), 'row', [(r, r ^ partner_...  14.1 us
    add x12, other arithmetic, pair_sum(): return keep + got.astype(jnp.float32) / scale  11.6 us
  transfers between devices with their start and end apart: 14, of which 10 were waited for; matrix products, arithmetic and copies ran while one was open for 13% of the time, Pallas kernels for 0%

profile of v4, /device:TPU:0, one launch (start us, length us, event | category | flops | bytes accessed | tf_op | source)
XLA Modules:
  0.0 366.4 jit_solution(3167640218355794286)
XLA Ops:
  7.2 6.4 %copy.22 = bf16[2048,1024]{0,1:T(8,128)(2,1)} copy(bf16[2048,1024]{1,0:T(8,128)(2,1)} %param.5) | data formatting | bytes 8388608 | tf_op args[0]
  13.6 4.8 %fusion.28 = (bf16[2048,2,1,256]{0,3,2,1:T(8,128)(2,1)}, bf16[2048,2,1,256]{0,3,2,1:T(8,128)(2,1)}) fusion(bf16[2048,2,2,256]{0,3,2,1:T(8,128)(2,1)} %bitcast.108), kind=kLoop, calls=%fused_computation.56 | loop fusion | bytes 8388608 | tf_op jit(solution)/shard_map/slice | solution.py:54
  19.2 3.8 %abs_reduce_fusion = bf16[]{:T(256)} fusion(bf16[2048,1,1024]{2,0,1:T(8,128)(2,1)} %param.6), kind=kLoop, calls=%fused_computation | loop fusion | flops 4194303 | bytes 4194306 | tf_op jit(solution)/shard_map/reduce_max | solution.py:48
  23.0 23.7 %pmax.7 = f32[]{:T(128)} all-reduce(bf16[]{:T(256)} %abs_reduce_fusion), channel_id=1, replica_groups=mesh['row'=8,'col'=4] {'row'}, use_global_device_ids=true, to_apply=%region_1.0 | all-reduce | flops 1 | bytes 6 | tf_op jit(solution)/shard_map/pmax | solution.py:48
  47.4 32.2 %all-gather.5.cloned.1.call-done = bf16[2048,2048]{0,1:T(8,128)(2,1)} async-done(((bf16[2048,512]{0,1:T(8,128)(2,1)}), bf16[2048,2048]{0,1:T(8,128)(2,1)}) %all-gather.5.cloned.1.call-update) | async-done | bytes 8388624 | tf_op jit(solution)/shard_map/all_gather | solution.py:55
  79.6 7.7 %fusion.12 = f32[2048,512]{1,0:T(8,128)S(1)} fusion(bf16[2048,2048]{0,1:T(8,128)(2,1)} %all-gather.5.cloned.1.call-done, bf16[2048,1024]{1,0:T(8,128)(2,1)} %bitcast.112), kind=kOutput, calls=%fused_computation.24 | convolution fusion | flops 4294967296 | bytes 14680064 | tf_op jit(solution)/shard_map/dot_general | solution.py:14
  90.8 4.5 %fusion.8 = f32[2048,512]{1,0:T(8,128)S(1)} fusion(bf16[2048,2048]{0,1:T(8,128)(2,1)S(1)} %copy-done.12, bf16[2048,1024]{1,0:T(8,128)(2,1)S(1)} %bitcast.114), kind=kOutput, calls=%fused_computation.20 | convolution fusion | flops 4294967296 | bytes 14680064 | tf_op jit(solution)/shard_map/dot_general | solution.py:14
  99.2 15.6 %collective-permute-done = f16[2,2,256,512]{3,2,1,0:T(8,128)(2,1)} collective-permute-done((f16[2,2,256,512]{3,2,1,0:T(8,128)(2,1)S(1)}, f16[2,2,256,512]{3,2,1,0:T(8,128)(2,1)}, u32[]{:S(2)}, u32[]{:S(2)}) %collective-permute-start) | collective-permute-done | bytes 1048608 | tf_op jit(solution)/shard_map/ppermute | solution.py:23
  119.5 4.3 %collective-permute-done.3 = f16[2,2,256,512]{3,2,1,0:T(8,128)(2,1)} collective-permute-done((f16[2,2,256,512]{3,2,1,0:T(8,128)(2,1)S(1)}, f16[2,2,256,512]{3,2,1,0:T(8,128)(2,1)}, u32[]{:S(2)}, u32[]{:S(2)}) %collective-permute-start.3) | collective-permute-done | bytes 1048608 | tf_op jit(solution)/shard_map/ppermute | solution.py:23
  128.3 2.4 collective-permute-start.4
  130.7 9.0 %collective-permute-done.1 = f16[2,256,512]{2,1,0:T(8,128)(2,1)} collective-permute-done((f16[2,256,512]{2,1,0:T(8,128)(2,1)}, f16[2,256,512]{2,1,0:T(8,128)(2,1)}, u32[]{:S(2)}, u32[]{:S(2)}) %collective-permute-start.1) | collective-permute-done | bytes 524320 | tf_op jit(solution)/shard_map/ppermute | solution.py:23
  141.0 7.9 %fusion.10 = f32[2048,512]{1,0:T(8,128)S(1)} fusion(bf16[2048,2048]{0,1:T(8,128)(2,1)} %all-gather.3.cloned.1.call-done, bf16[2048,1024]{1,0:T(8,128)(2,1)} %bitcast.113), kind=kOutput, calls=%fused_computation.22 | convolution fusion | flops 4294967296 | bytes 14680064 | tf_op jit(solution)/shard_map/dot_general | solution.py:14
  151.7 4.5 %fusion.6 = f32[2048,512]{1,0:T(8,128)S(1)} fusion(bf16[2048,2048]{0,1:T(8,128)(2,1)S(1)} %copy-done.11, bf16[2048,1024]{1,0:T(8,128)(2,1)S(1)} %bitcast.115), kind=kOutput, calls=%fused_computation.18 | convolution fusion | flops 4294967296 | bytes 14680064 | tf_op jit(solution)/shard_map/dot_general | solution.py:14
  165.5 2.5 collective-permute-start.2
  168.0 9.6 %collective-permute-done.6 = f16[2,2,256,512]{3,2,1,0:T(8,128)(2,1)} collective-permute-done((f16[2,2,256,512]{3,2,1,0:T(8,128)(2,1)}, f16[2,2,256,512]{3,2,1,0:T(8,128)(2,1)}, u32[]{:S(2)}, u32[]{:S(2)}) %collective-permute-start.6) | collective-permute-done | bytes 1048608 | tf_op jit(solution)/shard_map/ppermute | solution.py:23
  180.0 11.5 %collective-permute-done.9 = f16[2,2,256,512]{3,2,1,0:T(8,128)(2,1)} collective-permute-done((f16[2,2,256,512]{3,2,1,0:T(8,128)(2,1)}, f16[2,2,256,512]{3,2,1,0:T(8,128)(2,1)}, u32[]{:S(2)}, u32[]{:S(2)}) %collective-permute-start.9) | collective-permute-done | bytes 1048608 | tf_op jit(solution)/shard_map/ppermute | solution.py:23
  194.8 15.5 %collective-permute-done.7 = f16[2,256,512]{2,1,0:T(8,128)(2,1)S(1)} collective-permute-done((f16[2,256,512]{2,1,0:T(8,128)(2,1)S(1)}, f16[2,256,512]{2,1,0:T(8,128)(2,1)S(1)}, u32[]{:S(2)}, u32[]{:S(2)}) %collective-permute-start.7) | collective-permute-done | bytes 524320 | tf_op jit(solution)/shard_map/ppermute | solution.py:23
  210.6 15.0 %collective-permute-done.10 = f16[2,256,512]{2,1,0:T(8,128)(2,1)S(1)} collective-permute-done((f16[2,256,512]{2,1,0:T(8,128)(2,1)S(1)}, f16[2,256,512]{2,1,0:T(8,128)(2,1)S(1)}, u32[]{:S(2)}, u32[]{:S(2)}) %collective-permute-start.10) | collective-permute-done | bytes 524320 | tf_op jit(solution)/shard_map/ppermute | solution.py:23
  226.0 2.6 collective-permute-done.8
  228.8 3.5 collective-permute-done.11
  233.1 110.6 %shard_map.92 = (bf16[4096,1024]{1,0:T(8,128)(2,1)}, f32[512,1024]{1,0:T(8,128)S(1)}, f32[512,1024]{1,0:T(8,128)S(1)}, f32[1,512]{1,0:T(1,128)S(1)}, f32[1,1024]{1,0:T(1,128)S(1)}) custom-call(f32[512,1024]{1,0:T(8,128)S(1)} %get-tuple-element.38.grad, f32[8,512]{1,0:T(8,128)S(1)} %broadcast_in_dim.12.row_part, f32[8,1024]{1,0:T(8,128)S(1)} %broadcast_in_dim.13.col_part, ...), custom_call_target="tpu_custom_call" | custom-call | tf_op jit(solution)/shard_map/pallas_call | solution.py:254
  343.7 3.5 copy.29
  347.2 3.5 copy.30
  350.7 7.8 %copy.41 = bf16[4096,1,1024]{2,0,1:T(8,128)(2,1)} copy(bf16[4096,1,1024]{2,0,1:T(8,128)(2,1)} %bitcast.109) | data formatting | bytes 16777216
  (76 shorter events, 39.0 us)
Async XLA Ops:
  7.2 72.5 %all-gather.5.cloned.1.call-start = ((), (), s32[]{:S(2)}) async-start(), calls=%async_computation.1 | async-start | bytes 10485760 | tf_op jit(solution)/shard_map/all_gather | solution.py:55
  18.5 122.5 %all-gather.3.cloned.1.call-start = ((), (), s32[]{:S(2)}) async-start(), calls=%async_computation | async-start | bytes 10485760 | tf_op jit(solution)/shard_map/all_gather | solution.py:55
  79.6 11.2 %copy-start.1 = (bf16[2048,1,1024]{2,0,1:T(8,128)(2,1)S(1)}, bf16[2048,1,1024]{2,0,1:T(8,128)(2,1)}, u32[]{:S(2)}) copy-start(bf16[2048,1,1024]{2,0,1:T(8,128)(2,1)} %param.6) | copy-start | bytes 12582916
  79.6 11.2 %copy-start.12 = (bf16[2048,2048]{0,1:T(8,128)(2,1)S(1)}, bf16[2048,2048]{0,1:T(8,128)(2,1)}, u32[]{:S(2)}) copy-start(bf16[2048,2048]{0,1:T(8,128)(2,1)} %all-gather.5.cloned.1.call-done) | copy-start | bytes 25165828
  87.3 2.0 copy-start.8
  89.3 25.4 %collective-permute-start = (f16[2,2,256,512]{3,2,1,0:T(8,128)(2,1)S(1)}, f16[2,2,256,512]{3,2,1,0:T(8,128)(2,1)}, u32[]{:S(2)}, u32[]{:S(2)}) collective-permute-start(f16[2,2,256,512]{3,2,1,0:T(8,128)(2,1)S(1)} %fusion.14), channel_id=1, source_target_pairs={{0,4},{4,0},{8,12},{12,8},{16,20},{20,16},{24,28},{28,24},{1,5},{5... | collective-permute-start | bytes 3145736 | tf_op jit(solution)/shard_map/ppermute | solution.py:23
  95.3 2.0 copy-start.3
  97.6 26.2 %collective-permute-start.3 = (f16[2,2,256,512]{3,2,1,0:T(8,128)(2,1)S(1)}, f16[2,2,256,512]{3,2,1,0:T(8,128)(2,1)}, u32[]{:S(2)}, u32[]{:S(2)}) collective-permute-start(f16[2,2,256,512]{3,2,1,0:T(8,128)(2,1)S(1)} %fusion.15), channel_id=1, source_target_pairs={{0,8},{4,12},{8,0},{12,4},{16,24},{20,28},{24,16},{28,20},{1,9},{5... | collective-permute-start | bytes 3145736 | tf_op jit(solution)/shard_map/ppermute | solution.py:23
  118.0 21.7 %collective-permute-start.1 = (f16[2,256,512]{2,1,0:T(8,128)(2,1)}, f16[2,256,512]{2,1,0:T(8,128)(2,1)}, u32[]{:S(2)}, u32[]{:S(2)}) collective-permute-start(f16[2,256,512]{2,1,0:T(8,128)(2,1)} %fusion.22), channel_id=1, source_target_pairs={{0,8},{4,12},{8,0},{12,4},{16,24},{20,28},{24,16},{28,20},{1,9},{5... | collective-permute-start | bytes 1572872 | tf_op jit(solution)/shard_map/ppermute | solution.py:23
  128.3 34.7 %collective-permute-start.4 = (f16[2,256,512]{2,1,0:T(8,128)(2,1)}, f16[2,256,512]{2,1,0:T(8,128)(2,1)}, u32[]{:S(2)}, u32[]{:S(2)}) collective-permute-start(f16[2,256,512]{2,1,0:T(8,128)(2,1)} %fusion.20), channel_id=1, source_target_pairs={{0,16},{4,20},{8,24},{12,28},{16,0},{20,4},{24,8},{28,12},{1,17},{... | collective-permute-start | bytes 1572872 | tf_op jit(solution)/shard_map/ppermute | solution.py:23
  141.0 10.7 %copy-start.2 = (bf16[2048,1,1024]{2,0,1:T(8,128)(2,1)S(1)}, bf16[2048,1,1024]{2,0,1:T(8,128)(2,1)}, u32[]{:S(2)}) copy-start(bf16[2048,1,1024]{2,0,1:T(8,128)(2,1)} %param.6) | copy-start | bytes 12582916
  141.0 10.7 %copy-start.11 = (bf16[2048,2048]{0,1:T(8,128)(2,1)S(1)}, bf16[2048,2048]{0,1:T(8,128)(2,1)}, u32[]{:S(2)}) copy-start(bf16[2048,2048]{0,1:T(8,128)(2,1)} %all-gather.3.cloned.1.call-done) | copy-start | bytes 25165828
  148.9 2.3 copy-start.6
  151.2 26.4 %collective-permute-start.6 = (f16[2,2,256,512]{3,2,1,0:T(8,128)(2,1)}, f16[2,2,256,512]{3,2,1,0:T(8,128)(2,1)}, u32[]{:S(2)}, u32[]{:S(2)}) collective-permute-start(f16[2,2,256,512]{3,2,1,0:T(8,128)(2,1)} %fusion.16), channel_id=1, source_target_pairs={{0,4},{4,0},{8,12},{12,8},{16,20},{20,16},{24,28},{28,24},{1,5},{5... | collective-permute-start | bytes 3145736 | tf_op jit(solution)/shard_map/ppermute | solution.py:23
  156.3 2.0 copy-start.4
  159.5 32.0 %collective-permute-start.9 = (f16[2,2,256,512]{3,2,1,0:T(8,128)(2,1)}, f16[2,2,256,512]{3,2,1,0:T(8,128)(2,1)}, u32[]{:S(2)}, u32[]{:S(2)}) collective-permute-start(f16[2,2,256,512]{3,2,1,0:T(8,128)(2,1)} %fusion.17), channel_id=1, source_target_pairs={{0,8},{4,12},{8,0},{12,4},{16,24},{20,28},{24,16},{28,20},{1,9},{5... | collective-permute-start | bytes 3145736 | tf_op jit(solution)/shard_map/ppermute | solution.py:23
  163.1 14.5 %copy-start.7 = (f32[2048,512]{1,0:T(8,128)S(1)}, f32[2048,512]{1,0:T(8,128)}, u32[]{:S(2)}) copy-start(f32[2048,512]{1,0:T(8,128)} %copy-done.6) | copy-start | bytes 12582916
  164.9 29.9 %collective-permute-start.5 = (f16[256,512]{1,0:T(8,128)(2,1)S(1)}, f16[256,512]{1,0:T(8,128)(2,1)S(1)}, u32[]{:S(2)}, u32[]{:S(2)}) collective-permute-start(f16[256,512]{1,0:T(8,128)(2,1)S(1)} %fusion.25), channel_id=1, source_target_pairs={{0,4},{4,0},{8,12},{12,8},{16,20},{20,16},{24,28},{28,24},{1,5},{5... | collective-permute-start | bytes 786440 | tf_op jit(solution)/shard_map/ppermute | solution.py:23
  165.5 60.4 %collective-permute-start.2 = (f16[256,512]{1,0:T(8,128)(2,1)S(1)}, f16[256,512]{1,0:T(8,128)(2,1)S(1)}, u32[]{:S(2)}, u32[]{:S(2)}) collective-permute-start(f16[256,512]{1,0:T(8,128)(2,1)S(1)} %fusion.24), channel_id=1, source_target_pairs={{0,16},{4,20},{8,24},{12,28},{16,0},{20,4},{24,8},{28,12},{1,17},{... | collective-permute-start | bytes 786440 | tf_op jit(solution)/shard_map/ppermute | solution.py:23
  177.6 13.9 %copy-start.5 = (f32[2048,512]{1,0:T(8,128)S(1)}, f32[2048,512]{1,0:T(8,128)}, u32[]{:S(2)}) copy-start(f32[2048,512]{1,0:T(8,128)} %copy-done.4) | copy-start | bytes 12582916
  179.5 30.7 %collective-permute-start.7 = (f16[2,256,512]{2,1,0:T(8,128)(2,1)S(1)}, f16[2,256,512]{2,1,0:T(8,128)(2,1)S(1)}, u32[]{:S(2)}, u32[]{:S(2)}) collective-permute-start(f16[2,256,512]{2,1,0:T(8,128)(2,1)S(1)} %fusion.23), channel_id=1, source_target_pairs={{0,8},{4,12},{8,0},{12,4},{16,24},{20,28},{24,16},{28,20},{1,9},{5... | collective-permute-start | bytes 1572872 | tf_op jit(solution)/shard_map/ppermute | solution.py:23
  193.2 32.3 %collective-permute-start.10 = (f16[2,256,512]{2,1,0:T(8,128)(2,1)S(1)}, f16[2,256,512]{2,1,0:T(8,128)(2,1)S(1)}, u32[]{:S(2)}, u32[]{:S(2)}) collective-permute-start(f16[2,256,512]{2,1,0:T(8,128)(2,1)S(1)} %fusion.21), channel_id=1, source_target_pairs={{0,16},{4,20},{8,24},{12,28},{16,0},{20,4},{24,8},{28,12},{1,17},{... | collective-permute-start | bytes 1572872 | tf_op jit(solution)/shard_map/ppermute | solution.py:23
  210.5 18.2 %collective-permute-start.8 = (f16[256,512]{1,0:T(8,128)(2,1)S(1)}, f16[256,512]{1,0:T(8,128)(2,1)S(1)}, u32[]{:S(2)}, u32[]{:S(2)}) collective-permute-start(f16[256,512]{1,0:T(8,128)(2,1)S(1)} %fusion.26), channel_id=1, source_target_pairs={{0,16},{4,20},{8,24},{12,28},{16,0},{20,4},{24,8},{28,12},{1,17},{... | collective-permute-start | bytes 786440 | tf_op jit(solution)/shard_map/ppermute | solution.py:23
  225.8 6.4 %collective-permute-start.11 = (f16[256,512]{1,0:T(8,128)(2,1)S(1)}, f16[256,512]{1,0:T(8,128)(2,1)S(1)}, u32[]{:S(2)}, u32[]{:S(2)}) collective-permute-start(f16[256,512]{1,0:T(8,128)(2,1)S(1)} %fusion.27), channel_id=1, source_target_pairs={{0,4},{4,0},{8,12},{12,8},{16,20},{20,16},{24,28},{28,24},{1,5},{5... | collective-permute-start | bytes 786440 | tf_op jit(solution)/shard_map/ppermute | solution.py:23
  (3 other events, 2.7 us)
Sparse Core Ops, SparseCore 0:
  18.6 60.9 all-gather.4
  81.8 58.2 all-gather.2

commit v5 on v4

--- a/solution.py
+++ b/solution.py
@@ -47,14 +47,15 @@
     r = lax.axis_index("row")
     top = lax.pmax(jnp.max(jnp.abs(flat_out)).astype(jnp.float32), "row")
     scale = 16384.0 / (6.0 * tok * lax.axis_size("row") * jnp.maximum(top, 1e-30))
-    step = width // 4
+    parts = 4
+    step = width // (2 * parts)
     pieces = []
     sums = []
-    for k in range(2):
-        mine = acts.reshape(tok, 2, 2, step)[:, :, k].reshape(tok, 2 * step)
+    for k in range(parts):
+        mine = acts.reshape(tok, 2, parts, step)[:, :, k].reshape(tok, 2 * step)
         full = lax.all_gather(mine, "col", axis=1, tiled=True)
         half = cols // 2
-        if k == 1:
+        if k:
             full, sums[0] = lax.optimization_barrier((full, sums[0]))
             pieces.append([last_swap(sums[j], r, j == 0, scale) for j in range(2)])
         sums = []

time: 367 us -> 350 us (0.954)
  waiting for transfers between devices: 119 us -> 83.7 us
  starting transfers between devices: 14.2 us -> 39.2 us
  local copies, waits for them, and re-layouts: 37.2 us -> 29.1 us
  matrix products: 24.6 us -> 30.8 us
    ppermute x12 -> x24, starting transfers between devices: 14.1 us -> 39 us  [pair_sum(): lax.ppermute((give * scale).astype(jnp.float16), 'row', [(r, r ^ partner_...]
    all_gather x2 -> x4, waiting for transfers between devices: 32.2 us -> 7.63 us  [gradient_rows(): full = lax.all_gather(mine, 'col', axis=1, tiled=True)]
    ppermute x12 -> x24, waiting for transfers between devices: 86.6 us -> 74.6 us  [pair_sum(): lax.ppermute((give * scale).astype(jnp.float16), 'row', [(r, r ^ partner_...]
    unnamed x33 -> x37, local copies, waits for them, and re-layouts: 32.3 us -> 24.6 us
    dot_general x4 -> x8, matrix products: 24.6 us -> 30.8 us  [contract_tokens(): lax.dot_general(left, right, (((0,), (0,)), ((), ())), preferred_element_...]
    add x12 -> x24, other arithmetic: 11.6 us -> 8.75 us  [pair_sum(): return keep + got.astype(jnp.float32) / scale]
  transfers between devices with their start and end apart: 14 -> 28, of which waited for: 10 -> 17; matrix products, arithmetic and copies ran while one was open for 13% -> 14% of each run, Pallas kernels for 0% -> 0%
where the time goes in v5:
time: 350 us
  Pallas kernels  110 us (31%)
  waiting for transfers between devices  83.7 us (24%)
  starting transfers between devices  39.2 us (11%)
  matrix products  30.8 us (9%)
  local copies, waits for them, and re-layouts  29.1 us (8%)
  blocking collectives  23.7 us (7%)
  other arithmetic  17.9 us (5%)
  between operations  15 us (4%)
    pallas_call x1, Pallas kernels, tail(): pl.pallas_call(functools.partial(tail_kernel, rows_n, cols_n), out_shape=...  110 us
    ppermute x24, waiting for transfers between devices, pair_sum(): lax.ppermute((give * scale).astype(jnp.float16), 'row', [(r, r ^ partner_...  74.6 us
    ppermute x24, starting transfers between devices, pair_sum(): lax.ppermute((give * scale).astype(jnp.float16), 'row', [(r, r ^ partner_...  39 us
    dot_general x8, matrix products, contract_tokens(): lax.dot_general(left, right, (((0,), (0,)), ((), ())), preferred_element_...  30.8 us
    unnamed x37, local copies, waits for them, and re-layouts  24.6 us
    pmax x1, blocking collectives, gradient_rows(): top = lax.pmax(jnp.max(jnp.abs(flat_out)).astype(jnp.float32), 'row')  23.7 us
    add x24, other arithmetic, pair_sum(): return keep + got.astype(jnp.float32) / scale  8.75 us
    all_gather x4, waiting for transfers between devices, gradient_rows(): full = lax.all_gather(mine, 'col', axis=1, tiled=True)  7.63 us
  transfers between devices with their start and end apart: 28, of which 17 were waited for; matrix products, arithmetic and copies ran while one was open for 14% of the time, Pallas kernels for 0%

profile of v5, /device:TPU:0, one launch (start us, length us, event | category | flops | bytes accessed | tf_op | source)
XLA Modules:
  0.0 349.7 jit_solution(2911788887049847294)
XLA Ops:
  7.2 6.4 %copy.33 = bf16[2048,1024]{0,1:T(8,128)(2,1)} copy(bf16[2048,1024]{1,0:T(8,128)(2,1)} %param.5) | data formatting | bytes 8388608 | tf_op args[0]
  13.6 4.4 %fusion.53 = (bf16[2048,2,1,128]{0,3,2,1:T(8,128)(2,1)}, bf16[2048,2,1,128]{0,3,2,1:T(8,128)(2,1)}, bf16[2048,2,1,128]{0,3,2,1:T(8,128)(2,1)}, bf16[2048,2,1,128]{0,3,2,1:T(8,128)(2,1)}) fusion(bf16[2048,2,4,128]{0,3,2,1:T(8,128)(2,1)} %bitcast.190), kind=kLoop, calls=%fused_computation.107 | loop fusion | bytes 8388608 | tf_op jit(solution)/shard_map/slice | solution.py:55
  19.6 3.8 %abs_reduce_fusion = bf16[]{:T(256)} fusion(bf16[2048,1,1024]{2,0,1:T(8,128)(2,1)} %param.6), kind=kLoop, calls=%fused_computation | loop fusion | flops 4194303 | bytes 4194306 | tf_op jit(solution)/shard_map/reduce_max | solution.py:48
  23.3 23.7 %pmax.7 = f32[]{:T(128)} all-reduce(bf16[]{:T(256)} %abs_reduce_fusion), channel_id=1, replica_groups=mesh['row'=8,'col'=4] {'row'}, use_global_device_ids=true, to_apply=%region_1.0 | all-reduce | flops 1 | bytes 6 | tf_op jit(solution)/shard_map/pmax | solution.py:48
  47.8 7.6 %all-gather.7.cloned.1.call-done = bf16[2048,1024]{0,1:T(8,128)(2,1)} async-done(((bf16[2048,256]{0,1:T(8,128)(2,1)}), bf16[2048,1024]{0,1:T(8,128)(2,1)}) %all-gather.7.cloned.1.call-update) | async-done | bytes 4194320 | tf_op jit(solution)/shard_map/all_gather | solution.py:56
  55.4 5.3 %fusion.8 = f32[1024,512]{1,0:T(8,128)S(1)} fusion(bf16[2048,1024]{0,1:T(8,128)(2,1)} %all-gather.7.cloned.1.call-done, bf16[2048,1024]{1,0:T(8,128)(2,1)} %bitcast.192), kind=kOutput, calls=%fused_computation.12 | convolution fusion | flops 2147483648 | bytes 8388608 | tf_op jit(solution)/shard_map/dot_general | solution.py:14
  70.4 5.9 %collective-permute-done.3 = f16[2,2,128,512]{3,2,1,0:T(8,128)(2,1)} collective-permute-done((f16[2,2,128,512]{3,2,1,0:T(8,128)(2,1)}, f16[2,2,128,512]{3,2,1,0:T(8,128)(2,1)}, u32[]{:S(2)}, u32[]{:S(2)}) %collective-permute-start.3) | collective-permute-done | bytes 524320 | tf_op jit(solution)/shard_map/ppermute | solution.py:23
  83.2 9.1 %collective-permute-done.4 = f16[2,128,512]{2,1,0:T(8,128)(2,1)S(1)} collective-permute-done((f16[2,128,512]{2,1,0:T(8,128)(2,1)S(1)}, f16[2,128,512]{2,1,0:T(8,128)(2,1)S(1)}, u32[]{:S(2)}, u32[]{:S(2)}) %collective-permute-start.4) | collective-permute-done | bytes 262176 | tf_op jit(solution)/shard_map/ppermute | solution.py:23
  94.4 5.3 %fusion.6 = f32[1024,512]{1,0:T(8,128)S(1)} fusion(bf16[2048,1024]{0,1:T(8,128)(2,1)} %all-gather.5.cloned.1.call-done, bf16[2048,1024]{1,0:T(8,128)(2,1)} %bitcast.193), kind=kOutput, calls=%fused_computation.10 | convolution fusion | flops 2147483648 | bytes 8388608 | tf_op jit(solution)/shard_map/dot_general | solution.py:14
  103.9 3.9 %collective-permute-start.2 = (f16[128,512]{1,0:T(8,128)(2,1)S(1)}, f16[128,512]{1,0:T(8,128)(2,1)S(1)}, u32[]{:S(2)}, u32[]{:S(2)}) collective-permute-start(f16[128,512]{1,0:T(8,128)(2,1)S(1)} %fusion.45), channel_id=1, source_target_pairs={{0,16},{4,20},{8,24},{12,28},{16,0},{20,4},{24,8},{28,12},{1,17},{... | collective-permute-start | bytes 393224 | tf_op jit(solution)/shard_map/ppermute | solution.py:23
  107.9 6.0 %collective-permute-done.2 = f16[128,512]{1,0:T(8,128)(2,1)S(1)} collective-permute-done((f16[128,512]{1,0:T(8,128)(2,1)S(1)}, f16[128,512]{1,0:T(8,128)(2,1)S(1)}, u32[]{:S(2)}, u32[]{:S(2)}) %collective-permute-start.2) | collective-permute-done | bytes 131104 | tf_op jit(solution)/shard_map/ppermute | solution.py:23
  120.4 8.9 %collective-permute-done.10 = f16[2,128,512]{2,1,0:T(8,128)(2,1)S(1)} collective-permute-done((f16[2,128,512]{2,1,0:T(8,128)(2,1)S(1)}, f16[2,128,512]{2,1,0:T(8,128)(2,1)S(1)}, u32[]{:S(2)}, u32[]{:S(2)}) %collective-permute-start.10) | collective-permute-done | bytes 262176 | tf_op jit(solution)/shard_map/ppermute | solution.py:23
  130.2 5.3 %fusion.12 = f32[1024,512]{1,0:T(8,128)S(1)} fusion(bf16[2048,1024]{0,1:T(8,128)(2,1)} %all-gather.9.cloned.1.call-done, bf16[2048,1024]{1,0:T(8,128)(2,1)} %bitcast.194), kind=kOutput, calls=%fused_computation.16 | convolution fusion | flops 2147483648 | bytes 8388608 | tf_op jit(solution)/shard_map/dot_general | solution.py:14
  141.3 3.5 %collective-permute-start.8 = (f16[128,512]{1,0:T(8,128)(2,1)S(1)}, f16[128,512]{1,0:T(8,128)(2,1)S(1)}, u32[]{:S(2)}, u32[]{:S(2)}) collective-permute-start(f16[128,512]{1,0:T(8,128)(2,1)S(1)} %fusion.47), channel_id=1, source_target_pairs={{0,16},{4,20},{8,24},{12,28},{16,0},{20,4},{24,8},{28,12},{1,17},{... | collective-permute-start | bytes 393224 | tf_op jit(solution)/shard_map/ppermute | solution.py:23
  145.5 9.3 %collective-permute-done.8 = f16[128,512]{1,0:T(8,128)(2,1)S(1)} collective-permute-done((f16[128,512]{1,0:T(8,128)(2,1)S(1)}, f16[128,512]{1,0:T(8,128)(2,1)S(1)}, u32[]{:S(2)}, u32[]{:S(2)}) %collective-permute-start.8) | collective-permute-done | bytes 131104 | tf_op jit(solution)/shard_map/ppermute | solution.py:23
  155.8 4.2 %collective-permute-start.13 = (f16[2,128,512]{2,1,0:T(8,128)(2,1)S(1)}, f16[2,128,512]{2,1,0:T(8,128)(2,1)S(1)}, u32[]{:S(2)}, u32[]{:S(2)}) collective-permute-start(f16[2,128,512]{2,1,0:T(8,128)(2,1)S(1)} %fusion.43), channel_id=1, source_target_pairs={{0,8},{4,12},{8,0},{12,4},{16,24},{20,28},{24,16},{28,20},{1,9},{5... | collective-permute-start | bytes 786440 | tf_op jit(solution)/shard_map/ppermute | solution.py:23
  161.0 6.4 %collective-permute-done.13 = f16[2,128,512]{2,1,0:T(8,128)(2,1)S(1)} collective-permute-done((f16[2,128,512]{2,1,0:T(8,128)(2,1)S(1)}, f16[2,128,512]{2,1,0:T(8,128)(2,1)S(1)}, u32[]{:S(2)}, u32[]{:S(2)}) %collective-permute-start.13) | collective-permute-done | bytes 262176 | tf_op jit(solution)/shard_map/ppermute | solution.py:23
  168.2 5.3 %fusion.10 = f32[1024,512]{1,0:T(8,128)S(1)} fusion(bf16[2048,1024]{0,1:T(8,128)(2,1)} %all-gather.11.cloned.1.call-done, bf16[2048,1024]{1,0:T(8,128)(2,1)} %bitcast.195), kind=kOutput, calls=%fused_computation.14 | convolution fusion | flops 2147483648 | bytes 8388608 | tf_op jit(solution)/shard_map/dot_general | solution.py:14
  185.0 7.0 %collective-permute-done.18 = f16[2,2,128,512]{3,2,1,0:T(8,128)(2,1)S(1)} collective-permute-done((f16[2,2,128,512]{3,2,1,0:T(8,128)(2,1)S(1)}, f16[2,2,128,512]{3,2,1,0:T(8,128)(2,1)S(1)}, u32[]{:S(2)}, u32[]{:S(2)}) %collective-permute-start.18) | collective-permute-done | bytes 524320 | tf_op jit(solution)/shard_map/ppermute | solution.py:23
  201.7 9.4 %collective-permute-done.22 = f16[2,128,512]{2,1,0:T(8,128)(2,1)S(1)} collective-permute-done((f16[2,128,512]{2,1,0:T(8,128)(2,1)S(1)}, f16[2,128,512]{2,1,0:T(8,128)(2,1)S(1)}, u32[]{:S(2)}, u32[]{:S(2)}) %collective-permute-start.22) | collective-permute-done | bytes 262176 | tf_op jit(solution)/shard_map/ppermute | solution.py:23
  212.6 3.7 %collective-permute-done.23 = f16[128,512]{1,0:T(8,128)(2,1)S(1)} collective-permute-done((f16[128,512]{1,0:T(8,128)(2,1)S(1)}, f16[128,512]{1,0:T(8,128)(2,1)S(1)}, u32[]{:S(2)}, u32[]{:S(2)}) %collective-permute-start.23) | collective-permute-done | bytes 131104 | tf_op jit(solution)/shard_map/ppermute | solution.py:23
  217.1 110.2 %shard_map.92 = (bf16[4096,1024]{1,0:T(8,128)(2,1)}, f32[512,1024]{1,0:T(8,128)S(1)}, f32[512,1024]{1,0:T(8,128)S(1)}, f32[1,512]{1,0:T(1,128)S(1)}, f32[1,1024]{1,0:T(1,128)S(1)}) custom-call(f32[512,1024]{1,0:T(8,128)S(1)} %get-tuple-element.44.grad, f32[8,512]{1,0:T(8,128)S(1)} %broadcast_in_dim.12.row_part, f32[8,1024]{1,0:T(8,128)S(1)} %broadcast_in_dim.13.col_part, ...), custom_call_target="tpu_custom_call" | custom-call | tf_op jit(solution)/shard_map/pallas_call | solution.py:255
  327.3 3.5 copy.48
  334.2 7.8 %copy.70 = bf16[4096,1,1024]{2,0,1:T(8,128)(2,1)} copy(bf16[4096,1,1024]{2,0,1:T(8,128)(2,1)} %bitcast.191) | data formatting | bytes 16777216
  (139 shorter events, 68.7 us)
Async XLA Ops:
  7.2 48.2 %all-gather.7.cloned.1.call-start = ((), (), s32[]{:S(2)}) async-start(), calls=%async_computation.1 | async-start | bytes 5242880 | tf_op jit(solution)/shard_map/all_gather | solution.py:56
  18.0 76.4 %all-gather.5.cloned.1.call-start = ((), (), s32[]{:S(2)}) async-start(), calls=%async_computation | async-start | bytes 5242880 | tf_op jit(solution)/shard_map/all_gather | solution.py:56
  18.8 111.4 %all-gather.9.cloned.1.call-start = ((), (), s32[]{:S(2)}) async-start(), calls=%async_computation.2 | async-start | bytes 5242880 | tf_op jit(solution)/shard_map/all_gather | solution.py:56
  19.5 148.7 %all-gather.11.cloned.1.call-start = ((), (), s32[]{:S(2)}) async-start(), calls=%async_computation.3 | async-start | bytes 5242880 | tf_op jit(solution)/shard_map/all_gather | solution.py:56
  61.8 14.4 %collective-permute-start.3 = (f16[2,2,128,512]{3,2,1,0:T(8,128)(2,1)}, f16[2,2,128,512]{3,2,1,0:T(8,128)(2,1)}, u32[]{:S(2)}, u32[]{:S(2)}) collective-permute-start(f16[2,2,128,512]{3,2,1,0:T(8,128)(2,1)} %fusion.29), channel_id=1, source_target_pairs={{0,8},{4,12},{8,0},{12,4},{16,24},{20,28},{24,16},{28,20},{1,9},{5... | collective-permute-start | bytes 1572872 | tf_op jit(solution)/shard_map/ppermute | solution.py:23
  66.8 14.1 %collective-permute-start = (f16[2,2,128,512]{3,2,0,1:T(8,128)(2,1)}, f16[2,2,128,512]{3,2,0,1:T(8,128)(2,1)}, u32[]{:S(2)}, u32[]{:S(2)}) collective-permute-start(f16[2,2,128,512]{3,2,0,1:T(8,128)(2,1)} %fusion.26), channel_id=1, source_target_pairs={{0,4},{4,0},{8,12},{12,8},{16,20},{20,16},{24,28},{28,24},{1,5},{5... | collective-permute-start | bytes 1572872 | tf_op jit(solution)/shard_map/ppermute | solution.py:23
  77.9 14.4 %collective-permute-start.4 = (f16[2,128,512]{2,1,0:T(8,128)(2,1)S(1)}, f16[2,128,512]{2,1,0:T(8,128)(2,1)S(1)}, u32[]{:S(2)}, u32[]{:S(2)}) collective-permute-start(f16[2,128,512]{2,1,0:T(8,128)(2,1)S(1)} %fusion.38), channel_id=1, source_target_pairs={{0,16},{4,20},{8,24},{12,28},{16,0},{20,4},{24,8},{28,12},{1,17},{... | collective-permute-start | bytes 786440 | tf_op jit(solution)/shard_map/ppermute | solution.py:23
  82.2 12.1 %collective-permute-start.1 = (f16[2,128,512]{2,1,0:T(8,128)(2,1)S(1)}, f16[2,128,512]{2,1,0:T(8,128)(2,1)S(1)}, u32[]{:S(2)}, u32[]{:S(2)}) collective-permute-start(f16[2,128,512]{2,1,0:T(8,128)(2,1)S(1)} %fusion.37), channel_id=1, source_target_pairs={{0,8},{4,12},{8,0},{12,4},{16,24},{20,28},{24,16},{28,20},{1,9},{5... | collective-permute-start | bytes 786440 | tf_op jit(solution)/shard_map/ppermute | solution.py:23
  92.5 15.4 %collective-permute-start.5 = (f16[128,512]{1,0:T(8,128)(2,1)S(1)}, f16[128,512]{1,0:T(8,128)(2,1)S(1)}, u32[]{:S(2)}, u32[]{:S(2)}) collective-permute-start(f16[128,512]{1,0:T(8,128)(2,1)S(1)} %fusion.46), channel_id=1, source_target_pairs={{0,4},{4,0},{8,12},{12,8},{16,20},{20,16},{24,28},{28,24},{1,5},{5... | collective-permute-start | bytes 393224 | tf_op jit(solution)/shard_map/ppermute | solution.py:23
  99.9 15.0 %collective-permute-start.9 = (f16[2,2,128,512]{3,2,1,0:T(8,128)(2,1)S(1)}, f16[2,2,128,512]{3,2,1,0:T(8,128)(2,1)S(1)}, u32[]{:S(2)}, u32[]{:S(2)}) collective-permute-start(f16[2,2,128,512]{3,2,1,0:T(8,128)(2,1)S(1)} %fusion.30), channel_id=1, source_target_pairs={{0,8},{4,12},{8,0},{12,4},{16,24},{20,28},{24,16},{28,20},{1,9},{5... | collective-permute-start | bytes 1572872 | tf_op jit(solution)/shard_map/ppermute | solution.py:23
  102.5 15.8 %collective-permute-start.6 = (f16[2,2,128,512]{3,2,1,0:T(8,128)(2,1)S(1)}, f16[2,2,128,512]{3,2,1,0:T(8,128)(2,1)S(1)}, u32[]{:S(2)}, u32[]{:S(2)}) collective-permute-start(f16[2,2,128,512]{3,2,1,0:T(8,128)(2,1)S(1)} %fusion.27), channel_id=1, source_target_pairs={{0,4},{4,0},{8,12},{12,8},{16,20},{20,16},{24,28},{28,24},{1,5},{5... | collective-permute-start | bytes 1572872 | tf_op jit(solution)/shard_map/ppermute | solution.py:23
  103.9 10.0 %collective-permute-start.2 = (f16[128,512]{1,0:T(8,128)(2,1)S(1)}, f16[128,512]{1,0:T(8,128)(2,1)S(1)}, u32[]{:S(2)}, u32[]{:S(2)}) collective-permute-start(f16[128,512]{1,0:T(8,128)(2,1)S(1)} %fusion.45), channel_id=1, source_target_pairs={{0,16},{4,20},{8,24},{12,28},{16,0},{20,4},{24,8},{28,12},{1,17},{... | collective-permute-start | bytes 393224 | tf_op jit(solution)/shard_map/ppermute | solution.py:23
  115.1 14.1 %collective-permute-start.10 = (f16[2,128,512]{2,1,0:T(8,128)(2,1)S(1)}, f16[2,128,512]{2,1,0:T(8,128)(2,1)S(1)}, u32[]{:S(2)}, u32[]{:S(2)}) collective-permute-start(f16[2,128,512]{2,1,0:T(8,128)(2,1)S(1)} %fusion.39), channel_id=1, source_target_pairs={{0,16},{4,20},{8,24},{12,28},{16,0},{20,4},{24,8},{28,12},{1,17},{... | collective-permute-start | bytes 786440 | tf_op jit(solution)/shard_map/ppermute | solution.py:23
  118.6 11.4 %collective-permute-start.7 = (f16[2,128,512]{2,1,0:T(8,128)(2,1)S(1)}, f16[2,128,512]{2,1,0:T(8,128)(2,1)S(1)}, u32[]{:S(2)}, u32[]{:S(2)}) collective-permute-start(f16[2,128,512]{2,1,0:T(8,128)(2,1)S(1)} %fusion.42), channel_id=1, source_target_pairs={{0,8},{4,12},{8,0},{12,4},{16,24},{20,28},{24,16},{28,20},{1,9},{5... | collective-permute-start | bytes 786440 | tf_op jit(solution)/shard_map/ppermute | solution.py:23
  130.0 14.7 %collective-permute-start.11 = (f16[128,512]{1,0:T(8,128)(2,1)}, f16[128,512]{1,0:T(8,128)(2,1)S(1)}, u32[]{:S(2)}, u32[]{:S(2)}) collective-permute-start(f16[128,512]{1,0:T(8,128)(2,1)} %fusion.48), channel_id=1, source_target_pairs={{0,4},{4,0},{8,12},{12,8},{16,20},{20,16},{24,28},{28,24},{1,5},{5... | collective-permute-start | bytes 393224 | tf_op jit(solution)/shard_map/ppermute | solution.py:23
  135.7 19.9 %collective-permute-start.12 = (f16[2,2,128,512]{3,2,1,0:T(8,128)(2,1)S(1)}, f16[2,2,128,512]{3,2,1,0:T(8,128)(2,1)S(1)}, u32[]{:S(2)}, u32[]{:S(2)}) collective-permute-start(f16[2,2,128,512]{3,2,1,0:T(8,128)(2,1)S(1)} %fusion.28), channel_id=1, source_target_pairs={{0,4},{4,0},{8,12},{12,8},{16,20},{20,16},{24,28},{28,24},{1,5},{5... | collective-permute-start | bytes 1572872 | tf_op jit(solution)/shard_map/ppermute | solution.py:23
  140.4 19.6 %collective-permute-start.15 = (f16[2,2,128,512]{3,2,1,0:T(8,128)(2,1)S(1)}, f16[2,2,128,512]{3,2,1,0:T(8,128)(2,1)S(1)}, u32[]{:S(2)}, u32[]{:S(2)}) collective-permute-start(f16[2,2,128,512]{3,2,1,0:T(8,128)(2,1)S(1)} %fusion.31), channel_id=1, source_target_pairs={{0,8},{4,12},{8,0},{12,4},{16,24},{20,28},{24,16},{28,20},{1,9},{5... | collective-permute-start | bytes 1572872 | tf_op jit(solution)/shard_map/ppermute | solution.py:23
  141.3 13.6 %collective-permute-start.8 = (f16[128,512]{1,0:T(8,128)(2,1)S(1)}, f16[128,512]{1,0:T(8,128)(2,1)S(1)}, u32[]{:S(2)}, u32[]{:S(2)}) collective-permute-start(f16[128,512]{1,0:T(8,128)(2,1)S(1)} %fusion.47), channel_id=1, source_target_pairs={{0,16},{4,20},{8,24},{12,28},{16,0},{20,4},{24,8},{28,12},{1,17},{... | collective-permute-start | bytes 393224 | tf_op jit(solution)/shard_map/ppermute | solution.py:23
  155.8 11.5 %collective-permute-start.13 = (f16[2,128,512]{2,1,0:T(8,128)(2,1)S(1)}, f16[2,128,512]{2,1,0:T(8,128)(2,1)S(1)}, u32[]{:S(2)}, u32[]{:S(2)}) collective-permute-start(f16[2,128,512]{2,1,0:T(8,128)(2,1)S(1)} %fusion.43), channel_id=1, source_target_pairs={{0,8},{4,12},{8,0},{12,4},{16,24},{20,28},{24,16},{28,20},{1,9},{5... | collective-permute-start | bytes 786440 | tf_op jit(solution)/shard_map/ppermute | solution.py:23
  161.0 16.4 %collective-permute-start.16 = (f16[2,128,512]{2,1,0:T(8,128)(2,1)}, f16[2,128,512]{2,1,0:T(8,128)(2,1)}, u32[]{:S(2)}, u32[]{:S(2)}) collective-permute-start(f16[2,128,512]{2,1,0:T(8,128)(2,1)} %fusion.40), channel_id=1, source_target_pairs={{0,16},{4,20},{8,24},{12,28},{16,0},{20,4},{24,8},{28,12},{1,17},{... | collective-permute-start | bytes 786440 | tf_op jit(solution)/shard_map/ppermute | solution.py:23
  178.8 13.2 %collective-permute-start.18 = (f16[2,2,128,512]{3,2,1,0:T(8,128)(2,1)S(1)}, f16[2,2,128,512]{3,2,1,0:T(8,128)(2,1)S(1)}, u32[]{:S(2)}, u32[]{:S(2)}) collective-permute-start(f16[2,2,128,512]{3,2,1,0:T(8,128)(2,1)S(1)} %fusion.32), channel_id=1, source_target_pairs={{0,4},{4,0},{8,12},{12,8},{16,20},{20,16},{24,28},{28,24},{1,5},{5... | collective-permute-start | bytes 1572872 | tf_op jit(solution)/shard_map/ppermute | solution.py:23
  180.9 15.6 %collective-permute-start.21 = (f16[2,2,128,512]{3,2,1,0:T(8,128)(2,1)S(1)}, f16[2,2,128,512]{3,2,1,0:T(8,128)(2,1)S(1)}, u32[]{:S(2)}, u32[]{:S(2)}) collective-permute-start(f16[2,2,128,512]{3,2,1,0:T(8,128)(2,1)S(1)} %fusion.33), channel_id=1, source_target_pairs={{0,8},{4,12},{8,0},{12,4},{16,24},{20,28},{24,16},{28,20},{1,9},{5... | collective-permute-start | bytes 1572872 | tf_op jit(solution)/shard_map/ppermute | solution.py:23
  196.8 14.4 %collective-permute-start.22 = (f16[2,128,512]{2,1,0:T(8,128)(2,1)S(1)}, f16[2,128,512]{2,1,0:T(8,128)(2,1)S(1)}, u32[]{:S(2)}, u32[]{:S(2)}) collective-permute-start(f16[2,128,512]{2,1,0:T(8,128)(2,1)S(1)} %fusion.41), channel_id=1, source_target_pairs={{0,16},{4,20},{8,24},{12,28},{16,0},{20,4},{24,8},{28,12},{1,17},{... | collective-permute-start | bytes 786440 | tf_op jit(solution)/shard_map/ppermute | solution.py:23
  201.0 11.5 %collective-permute-start.20 = (f16[128,512]{1,0:T(8,128)(2,1)S(1)}, f16[128,512]{1,0:T(8,128)(2,1)S(1)}, u32[]{:S(2)}, u32[]{:S(2)}) collective-permute-start(f16[128,512]{1,0:T(8,128)(2,1)S(1)} %fusion.51), channel_id=1, source_target_pairs={{0,16},{4,20},{8,24},{12,28},{16,0},{20,4},{24,8},{28,12},{1,17},{... | collective-permute-start | bytes 393224 | tf_op jit(solution)/shard_map/ppermute | solution.py:23
  (19 other events, 148.1 us)
Sparse Core Ops, SparseCore 0:
  18.1 37.1 all-gather.6
  56.9 34.4 all-gather.4
  93.0 34.4 all-gather.8
  129.5 34.4 all-gather.10

commit v6 on v5

--- a/solution.py
+++ b/solution.py
@@ -68,7 +68,7 @@
 
 
 MESH = pl.DeviceIdType.MESH
-CHUNK = 32
+CHUNK = 16
 
 
 def exchange(axis, n, source, slots, send, recv):
@@ -160,10 +160,10 @@
         return carry
 
     first = height * 3 // 16
-    cuts = (0, first, (height + first) // 2, height)
+    cuts = (0, first, height * 13 // 32, height * 5 // 8, height * 13 // 16, height)
 
     def item(zs, ys, half, way):
-        number = (zs * 2 + ys) * 3 + half
+        number = (zs * 2 + ys) * 5 + half
         begins = pl.multiple_of((zs * 2 + ys) * height + cuts[half], 16)
         place = fresh.at[pl.ds(begins, cuts[half + 1] - cuts[half])]
         target = r + (1 - 2 * y) if way == 0 else (r + 2 if way == 1 else r - 2)
@@ -194,8 +194,8 @@
     item(z, y, 0, 0).start()
     for way in (1, 2):
         along(z, y, 0, way, begin)
-    lax.fori_loop(cuts[1] // CHUNK, height // CHUNK, finished, 0)
-    for half in (1, 2):
+    for half in range(1, 5):
+        lax.fori_loop(cuts[half] // CHUNK, cuts[half + 1] // CHUNK, finished, 0)
         for way in (1, 2):
             along(z, y, half, way, begin)
         item(z, y, half, 0).start()
@@ -203,7 +203,7 @@
     for way in (1, 2):
         along(z, 1 - y, 0, way, begin)
 
-    kinds = ((y, 0), (y, 1), (y, 2), (1 - y, 0))
+    kinds = ((y, 0), (y, 1), (y, 2), (y, 3), (y, 4), (1 - y, 0))
 
     def each(k, way, do):
         zs = z - k if way == 1 else z + k
@@ -226,7 +226,7 @@
     for k in range(depth):
         for way in (1, 2) if k else (1,):
             def last(zs):
-                for half in (1, 2):
+                for half in range(1, 5):
                     arrived(item(zs, 1 - y, half, 0))
                     sent(item(zs, y, half, 0))
 
@@ -251,7 +251,7 @@
 
     vmem = pl.BlockSpec(memory_space=pltpu.VMEM)
     dma = pltpu.SemaphoreType.DMA
-    items = rows_n * 3
+    items = rows_n * 5
     return pl.pallas_call(
         functools.partial(tail_kernel, rows_n, cols_n),
         out_shape=(

time: 350 us -> 348 us (level)
  transfers between devices with their start and end apart: 28 -> 28, of which waited for: 17 -> 17; matrix products, arithmetic and copies ran while one was open for 14% -> 15% of each run, Pallas kernels for 0% -> 0%
where the time goes in v6:
time: 348 us; the launch traced here: 347 us
  Pallas kernels  108 us (31%)
  waiting for transfers between devices  83.7 us (24%)
  starting transfers between devices  39.2 us (11%)
  matrix products  30.8 us (9%)
  local copies, waits for them, and re-layouts  29.1 us (8%)
  blocking collectives  23.7 us (7%)
  other arithmetic  17.9 us (5%)
  between operations  15 us (4%)
    pallas_call x1, Pallas kernels, tail(): pl.pallas_call(functools.partial(tail_kernel, rows_n, cols_n), out_shape=...  108 us
    ppermute x24, waiting for transfers between devices, pair_sum(): lax.ppermute((give * scale).astype(jnp.float16), 'row', [(r, r ^ partner_...  74.6 us
    ppermute x24, starting transfers between devices, pair_sum(): lax.ppermute((give * scale).astype(jnp.float16), 'row', [(r, r ^ partner_...  39 us
    dot_general x8, matrix products, contract_tokens(): lax.dot_general(left, right, (((0,), (0,)), ((), ())), preferred_element_...  30.8 us
    unnamed x37, local copies, waits for them, and re-layouts  24.6 us
    pmax x1, blocking collectives, gradient_rows(): top = lax.pmax(jnp.max(jnp.abs(flat_out)).astype(jnp.float32), 'row')  23.7 us
    add x24, other arithmetic, pair_sum(): return keep + got.astype(jnp.float32) / scale  8.75 us
    all_gather x4, waiting for transfers between devices, gradient_rows(): full = lax.all_gather(mine, 'col', axis=1, tiled=True)  7.63 us
  transfers between devices with their start and end apart: 28, of which 17 were waited for; matrix products, arithmetic and copies ran while one was open for 15% of the time, Pallas kernels for 0%

profile of v6, /device:TPU:0, one launch (start us, length us, event | category | flops | bytes accessed | tf_op | source)
XLA Modules:
  0.0 347.4 jit_solution(17727412187231956567)
XLA Ops:
  7.2 6.4 %copy.33 = bf16[2048,1024]{0,1:T(8,128)(2,1)} copy(bf16[2048,1024]{1,0:T(8,128)(2,1)} %param.5) | data formatting | bytes 8388608 | tf_op args[0]
  13.6 4.4 %fusion.53 = (bf16[2048,2,1,128]{0,3,2,1:T(8,128)(2,1)}, bf16[2048,2,1,128]{0,3,2,1:T(8,128)(2,1)}, bf16[2048,2,1,128]{0,3,2,1:T(8,128)(2,1)}, bf16[2048,2,1,128]{0,3,2,1:T(8,128)(2,1)}) fusion(bf16[2048,2,4,128]{0,3,2,1:T(8,128)(2,1)} %bitcast.190), kind=kLoop, calls=%fused_computation.107 | loop fusion | bytes 8388608 | tf_op jit(solution)/shard_map/slice | solution.py:55
  19.6 3.8 %abs_reduce_fusion = bf16[]{:T(256)} fusion(bf16[2048,1,1024]{2,0,1:T(8,128)(2,1)} %param.6), kind=kLoop, calls=%fused_computation | loop fusion | flops 4194303 | bytes 4194306 | tf_op jit(solution)/shard_map/reduce_max | solution.py:48
  23.3 23.7 %pmax.7 = f32[]{:T(128)} all-reduce(bf16[]{:T(256)} %abs_reduce_fusion), channel_id=1, replica_groups=mesh['row'=8,'col'=4] {'row'}, use_global_device_ids=true, to_apply=%region_1.0 | all-reduce | flops 1 | bytes 6 | tf_op jit(solution)/shard_map/pmax | solution.py:48
  47.8 7.6 %all-gather.7.cloned.1.call-done = bf16[2048,1024]{0,1:T(8,128)(2,1)} async-done(((bf16[2048,256]{0,1:T(8,128)(2,1)}), bf16[2048,1024]{0,1:T(8,128)(2,1)}) %all-gather.7.cloned.1.call-update) | async-done | bytes 4194320 | tf_op jit(solution)/shard_map/all_gather | solution.py:56
  55.4 5.3 %fusion.8 = f32[1024,512]{1,0:T(8,128)S(1)} fusion(bf16[2048,1024]{0,1:T(8,128)(2,1)} %all-gather.7.cloned.1.call-done, bf16[2048,1024]{1,0:T(8,128)(2,1)} %bitcast.192), kind=kOutput, calls=%fused_computation.12 | convolution fusion | flops 2147483648 | bytes 8388608 | tf_op jit(solution)/shard_map/dot_general | solution.py:14
  70.4 5.9 %collective-permute-done.3 = f16[2,2,128,512]{3,2,1,0:T(8,128)(2,1)} collective-permute-done((f16[2,2,128,512]{3,2,1,0:T(8,128)(2,1)}, f16[2,2,128,512]{3,2,1,0:T(8,128)(2,1)}, u32[]{:S(2)}, u32[]{:S(2)}) %collective-permute-start.3) | collective-permute-done | bytes 524320 | tf_op jit(solution)/shard_map/ppermute | solution.py:23
  83.2 9.1 %collective-permute-done.4 = f16[2,128,512]{2,1,0:T(8,128)(2,1)S(1)} collective-permute-done((f16[2,128,512]{2,1,0:T(8,128)(2,1)S(1)}, f16[2,128,512]{2,1,0:T(8,128)(2,1)S(1)}, u32[]{:S(2)}, u32[]{:S(2)}) %collective-permute-start.4) | collective-permute-done | bytes 262176 | tf_op jit(solution)/shard_map/ppermute | solution.py:23
  94.4 5.3 %fusion.6 = f32[1024,512]{1,0:T(8,128)S(1)} fusion(bf16[2048,1024]{0,1:T(8,128)(2,1)} %all-gather.5.cloned.1.call-done, bf16[2048,1024]{1,0:T(8,128)(2,1)} %bitcast.193), kind=kOutput, calls=%fused_computation.10 | convolution fusion | flops 2147483648 | bytes 8388608 | tf_op jit(solution)/shard_map/dot_general | solution.py:14
  103.9 3.9 %collective-permute-start.2 = (f16[128,512]{1,0:T(8,128)(2,1)S(1)}, f16[128,512]{1,0:T(8,128)(2,1)S(1)}, u32[]{:S(2)}, u32[]{:S(2)}) collective-permute-start(f16[128,512]{1,0:T(8,128)(2,1)S(1)} %fusion.45), channel_id=1, source_target_pairs={{0,16},{4,20},{8,24},{12,28},{16,0},{20,4},{24,8},{28,12},{1,17},{... | collective-permute-start | bytes 393224 | tf_op jit(solution)/shard_map/ppermute | solution.py:23
  107.9 6.0 %collective-permute-done.2 = f16[128,512]{1,0:T(8,128)(2,1)S(1)} collective-permute-done((f16[128,512]{1,0:T(8,128)(2,1)S(1)}, f16[128,512]{1,0:T(8,128)(2,1)S(1)}, u32[]{:S(2)}, u32[]{:S(2)}) %collective-permute-start.2) | collective-permute-done | bytes 131104 | tf_op jit(solution)/shard_map/ppermute | solution.py:23
  120.4 8.9 %collective-permute-done.10 = f16[2,128,512]{2,1,0:T(8,128)(2,1)S(1)} collective-permute-done((f16[2,128,512]{2,1,0:T(8,128)(2,1)S(1)}, f16[2,128,512]{2,1,0:T(8,128)(2,1)S(1)}, u32[]{:S(2)}, u32[]{:S(2)}) %collective-permute-start.10) | collective-permute-done | bytes 262176 | tf_op jit(solution)/shard_map/ppermute | solution.py:23
  130.2 5.3 %fusion.12 = f32[1024,512]{1,0:T(8,128)S(1)} fusion(bf16[2048,1024]{0,1:T(8,128)(2,1)} %all-gather.9.cloned.1.call-done, bf16[2048,1024]{1,0:T(8,128)(2,1)} %bitcast.194), kind=kOutput, calls=%fused_computation.16 | convolution fusion | flops 2147483648 | bytes 8388608 | tf_op jit(solution)/shard_map/dot_general | solution.py:14
  141.3 3.5 %collective-permute-start.8 = (f16[128,512]{1,0:T(8,128)(2,1)S(1)}, f16[128,512]{1,0:T(8,128)(2,1)S(1)}, u32[]{:S(2)}, u32[]{:S(2)}) collective-permute-start(f16[128,512]{1,0:T(8,128)(2,1)S(1)} %fusion.47), channel_id=1, source_target_pairs={{0,16},{4,20},{8,24},{12,28},{16,0},{20,4},{24,8},{28,12},{1,17},{... | collective-permute-start | bytes 393224 | tf_op jit(solution)/shard_map/ppermute | solution.py:23
  145.5 9.3 %collective-permute-done.8 = f16[128,512]{1,0:T(8,128)(2,1)S(1)} collective-permute-done((f16[128,512]{1,0:T(8,128)(2,1)S(1)}, f16[128,512]{1,0:T(8,128)(2,1)S(1)}, u32[]{:S(2)}, u32[]{:S(2)}) %collective-permute-start.8) | collective-permute-done | bytes 131104 | tf_op jit(solution)/shard_map/ppermute | solution.py:23
  155.8 4.2 %collective-permute-start.13 = (f16[2,128,512]{2,1,0:T(8,128)(2,1)S(1)}, f16[2,128,512]{2,1,0:T(8,128)(2,1)S(1)}, u32[]{:S(2)}, u32[]{:S(2)}) collective-permute-start(f16[2,128,512]{2,1,0:T(8,128)(2,1)S(1)} %fusion.43), channel_id=1, source_target_pairs={{0,8},{4,12},{8,0},{12,4},{16,24},{20,28},{24,16},{28,20},{1,9},{5... | collective-permute-start | bytes 786440 | tf_op jit(solution)/shard_map/ppermute | solution.py:23
  161.0 6.4 %collective-permute-done.13 = f16[2,128,512]{2,1,0:T(8,128)(2,1)S(1)} collective-permute-done((f16[2,128,512]{2,1,0:T(8,128)(2,1)S(1)}, f16[2,128,512]{2,1,0:T(8,128)(2,1)S(1)}, u32[]{:S(2)}, u32[]{:S(2)}) %collective-permute-start.13) | collective-permute-done | bytes 262176 | tf_op jit(solution)/shard_map/ppermute | solution.py:23
  168.2 5.3 %fusion.10 = f32[1024,512]{1,0:T(8,128)S(1)} fusion(bf16[2048,1024]{0,1:T(8,128)(2,1)} %all-gather.11.cloned.1.call-done, bf16[2048,1024]{1,0:T(8,128)(2,1)} %bitcast.195), kind=kOutput, calls=%fused_computation.14 | convolution fusion | flops 2147483648 | bytes 8388608 | tf_op jit(solution)/shard_map/dot_general | solution.py:14
  185.0 7.0 %collective-permute-done.18 = f16[2,2,128,512]{3,2,1,0:T(8,128)(2,1)S(1)} collective-permute-done((f16[2,2,128,512]{3,2,1,0:T(8,128)(2,1)S(1)}, f16[2,2,128,512]{3,2,1,0:T(8,128)(2,1)S(1)}, u32[]{:S(2)}, u32[]{:S(2)}) %collective-permute-start.18) | collective-permute-done | bytes 524320 | tf_op jit(solution)/shard_map/ppermute | solution.py:23
  201.7 9.4 %collective-permute-done.22 = f16[2,128,512]{2,1,0:T(8,128)(2,1)S(1)} collective-permute-done((f16[2,128,512]{2,1,0:T(8,128)(2,1)S(1)}, f16[2,128,512]{2,1,0:T(8,128)(2,1)S(1)}, u32[]{:S(2)}, u32[]{:S(2)}) %collective-permute-start.22) | collective-permute-done | bytes 262176 | tf_op jit(solution)/shard_map/ppermute | solution.py:23
  212.6 3.7 %collective-permute-done.23 = f16[128,512]{1,0:T(8,128)(2,1)S(1)} collective-permute-done((f16[128,512]{1,0:T(8,128)(2,1)S(1)}, f16[128,512]{1,0:T(8,128)(2,1)S(1)}, u32[]{:S(2)}, u32[]{:S(2)}) %collective-permute-start.23) | collective-permute-done | bytes 131104 | tf_op jit(solution)/shard_map/ppermute | solution.py:23
  217.1 107.9 %shard_map.92 = (bf16[4096,1024]{1,0:T(8,128)(2,1)}, f32[512,1024]{1,0:T(8,128)S(1)}, f32[512,1024]{1,0:T(8,128)S(1)}, f32[1,512]{1,0:T(1,128)S(1)}, f32[1,1024]{1,0:T(1,128)S(1)}) custom-call(f32[512,1024]{1,0:T(8,128)S(1)} %get-tuple-element.44.grad, f32[8,512]{1,0:T(8,128)S(1)} %broadcast_in_dim.12.row_part, f32[8,1024]{1,0:T(8,128)S(1)} %broadcast_in_dim.13.col_part, ...), custom_call_target="tpu_custom_call" | custom-call | tf_op jit(solution)/shard_map/pallas_call | solution.py:255
  325.0 3.5 %copy.48 = f32[512,1,1024]{2,1,0:T(1,128)} copy(f32[512,1,1024]{2,0,1:T(8,128)S(1)} %bitcast.189) | data formatting | bytes 4194304
  332.0 7.8 %copy.70 = bf16[4096,1,1024]{2,0,1:T(8,128)(2,1)} copy(bf16[4096,1,1024]{2,0,1:T(8,128)(2,1)} %bitcast.191) | data formatting | bytes 16777216
  (139 shorter events, 68.7 us)
Async XLA Ops:
  7.2 48.2 %all-gather.7.cloned.1.call-start = ((), (), s32[]{:S(2)}) async-start(), calls=%async_computation.1 | async-start | bytes 5242880 | tf_op jit(solution)/shard_map/all_gather | solution.py:56
  18.0 76.4 %all-gather.5.cloned.1.call-start = ((), (), s32[]{:S(2)}) async-start(), calls=%async_computation | async-start | bytes 5242880 | tf_op jit(solution)/shard_map/all_gather | solution.py:56
  18.8 111.4 %all-gather.9.cloned.1.call-start = ((), (), s32[]{:S(2)}) async-start(), calls=%async_computation.2 | async-start | bytes 5242880 | tf_op jit(solution)/shard_map/all_gather | solution.py:56
  19.5 148.7 %all-gather.11.cloned.1.call-start = ((), (), s32[]{:S(2)}) async-start(), calls=%async_computation.3 | async-start | bytes 5242880 | tf_op jit(solution)/shard_map/all_gather | solution.py:56
  61.8 14.4 %collective-permute-start.3 = (f16[2,2,128,512]{3,2,1,0:T(8,128)(2,1)}, f16[2,2,128,512]{3,2,1,0:T(8,128)(2,1)}, u32[]{:S(2)}, u32[]{:S(2)}) collective-permute-start(f16[2,2,128,512]{3,2,1,0:T(8,128)(2,1)} %fusion.29), channel_id=1, source_target_pairs={{0,8},{4,12},{8,0},{12,4},{16,24},{20,28},{24,16},{28,20},{1,9},{5... | collective-permute-start | bytes 1572872 | tf_op jit(solution)/shard_map/ppermute | solution.py:23
  66.8 14.1 %collective-permute-start = (f16[2,2,128,512]{3,2,0,1:T(8,128)(2,1)}, f16[2,2,128,512]{3,2,0,1:T(8,128)(2,1)}, u32[]{:S(2)}, u32[]{:S(2)}) collective-permute-start(f16[2,2,128,512]{3,2,0,1:T(8,128)(2,1)} %fusion.26), channel_id=1, source_target_pairs={{0,4},{4,0},{8,12},{12,8},{16,20},{20,16},{24,28},{28,24},{1,5},{5... | collective-permute-start | bytes 1572872 | tf_op jit(solution)/shard_map/ppermute | solution.py:23
  77.9 14.4 %collective-permute-start.4 = (f16[2,128,512]{2,1,0:T(8,128)(2,1)S(1)}, f16[2,128,512]{2,1,0:T(8,128)(2,1)S(1)}, u32[]{:S(2)}, u32[]{:S(2)}) collective-permute-start(f16[2,128,512]{2,1,0:T(8,128)(2,1)S(1)} %fusion.38), channel_id=1, source_target_pairs={{0,16},{4,20},{8,24},{12,28},{16,0},{20,4},{24,8},{28,12},{1,17},{... | collective-permute-start | bytes 786440 | tf_op jit(solution)/shard_map/ppermute | solution.py:23
  82.2 12.1 %collective-permute-start.1 = (f16[2,128,512]{2,1,0:T(8,128)(2,1)S(1)}, f16[2,128,512]{2,1,0:T(8,128)(2,1)S(1)}, u32[]{:S(2)}, u32[]{:S(2)}) collective-permute-start(f16[2,128,512]{2,1,0:T(8,128)(2,1)S(1)} %fusion.37), channel_id=1, source_target_pairs={{0,8},{4,12},{8,0},{12,4},{16,24},{20,28},{24,16},{28,20},{1,9},{5... | collective-permute-start | bytes 786440 | tf_op jit(solution)/shard_map/ppermute | solution.py:23
  92.5 15.4 %collective-permute-start.5 = (f16[128,512]{1,0:T(8,128)(2,1)S(1)}, f16[128,512]{1,0:T(8,128)(2,1)S(1)}, u32[]{:S(2)}, u32[]{:S(2)}) collective-permute-start(f16[128,512]{1,0:T(8,128)(2,1)S(1)} %fusion.46), channel_id=1, source_target_pairs={{0,4},{4,0},{8,12},{12,8},{16,20},{20,16},{24,28},{28,24},{1,5},{5... | collective-permute-start | bytes 393224 | tf_op jit(solution)/shard_map/ppermute | solution.py:23
  99.9 15.0 %collective-permute-start.9 = (f16[2,2,128,512]{3,2,1,0:T(8,128)(2,1)S(1)}, f16[2,2,128,512]{3,2,1,0:T(8,128)(2,1)S(1)}, u32[]{:S(2)}, u32[]{:S(2)}) collective-permute-start(f16[2,2,128,512]{3,2,1,0:T(8,128)(2,1)S(1)} %fusion.30), channel_id=1, source_target_pairs={{0,8},{4,12},{8,0},{12,4},{16,24},{20,28},{24,16},{28,20},{1,9},{5... | collective-permute-start | bytes 1572872 | tf_op jit(solution)/shard_map/ppermute | solution.py:23
  102.5 15.8 %collective-permute-start.6 = (f16[2,2,128,512]{3,2,1,0:T(8,128)(2,1)S(1)}, f16[2,2,128,512]{3,2,1,0:T(8,128)(2,1)S(1)}, u32[]{:S(2)}, u32[]{:S(2)}) collective-permute-start(f16[2,2,128,512]{3,2,1,0:T(8,128)(2,1)S(1)} %fusion.27), channel_id=1, source_target_pairs={{0,4},{4,0},{8,12},{12,8},{16,20},{20,16},{24,28},{28,24},{1,5},{5... | collective-permute-start | bytes 1572872 | tf_op jit(solution)/shard_map/ppermute | solution.py:23
  103.9 10.0 %collective-permute-start.2 = (f16[128,512]{1,0:T(8,128)(2,1)S(1)}, f16[128,512]{1,0:T(8,128)(2,1)S(1)}, u32[]{:S(2)}, u32[]{:S(2)}) collective-permute-start(f16[128,512]{1,0:T(8,128)(2,1)S(1)} %fusion.45), channel_id=1, source_target_pairs={{0,16},{4,20},{8,24},{12,28},{16,0},{20,4},{24,8},{28,12},{1,17},{... | collective-permute-start | bytes 393224 | tf_op jit(solution)/shard_map/ppermute | solution.py:23
  115.1 14.1 %collective-permute-start.10 = (f16[2,128,512]{2,1,0:T(8,128)(2,1)S(1)}, f16[2,128,512]{2,1,0:T(8,128)(2,1)S(1)}, u32[]{:S(2)}, u32[]{:S(2)}) collective-permute-start(f16[2,128,512]{2,1,0:T(8,128)(2,1)S(1)} %fusion.39), channel_id=1, source_target_pairs={{0,16},{4,20},{8,24},{12,28},{16,0},{20,4},{24,8},{28,12},{1,17},{... | collective-permute-start | bytes 786440 | tf_op jit(solution)/shard_map/ppermute | solution.py:23
  118.6 11.4 %collective-permute-start.7 = (f16[2,128,512]{2,1,0:T(8,128)(2,1)S(1)}, f16[2,128,512]{2,1,0:T(8,128)(2,1)S(1)}, u32[]{:S(2)}, u32[]{:S(2)}) collective-permute-start(f16[2,128,512]{2,1,0:T(8,128)(2,1)S(1)} %fusion.42), channel_id=1, source_target_pairs={{0,8},{4,12},{8,0},{12,4},{16,24},{20,28},{24,16},{28,20},{1,9},{5... | collective-permute-start | bytes 786440 | tf_op jit(solution)/shard_map/ppermute | solution.py:23
  130.0 14.7 %collective-permute-start.11 = (f16[128,512]{1,0:T(8,128)(2,1)}, f16[128,512]{1,0:T(8,128)(2,1)S(1)}, u32[]{:S(2)}, u32[]{:S(2)}) collective-permute-start(f16[128,512]{1,0:T(8,128)(2,1)} %fusion.48), channel_id=1, source_target_pairs={{0,4},{4,0},{8,12},{12,8},{16,20},{20,16},{24,28},{28,24},{1,5},{5... | collective-permute-start | bytes 393224 | tf_op jit(solution)/shard_map/ppermute | solution.py:23
  135.7 19.9 %collective-permute-start.12 = (f16[2,2,128,512]{3,2,1,0:T(8,128)(2,1)S(1)}, f16[2,2,128,512]{3,2,1,0:T(8,128)(2,1)S(1)}, u32[]{:S(2)}, u32[]{:S(2)}) collective-permute-start(f16[2,2,128,512]{3,2,1,0:T(8,128)(2,1)S(1)} %fusion.28), channel_id=1, source_target_pairs={{0,4},{4,0},{8,12},{12,8},{16,20},{20,16},{24,28},{28,24},{1,5},{5... | collective-permute-start | bytes 1572872 | tf_op jit(solution)/shard_map/ppermute | solution.py:23
  140.4 19.6 %collective-permute-start.15 = (f16[2,2,128,512]{3,2,1,0:T(8,128)(2,1)S(1)}, f16[2,2,128,512]{3,2,1,0:T(8,128)(2,1)S(1)}, u32[]{:S(2)}, u32[]{:S(2)}) collective-permute-start(f16[2,2,128,512]{3,2,1,0:T(8,128)(2,1)S(1)} %fusion.31), channel_id=1, source_target_pairs={{0,8},{4,12},{8,0},{12,4},{16,24},{20,28},{24,16},{28,20},{1,9},{5... | collective-permute-start | bytes 1572872 | tf_op jit(solution)/shard_map/ppermute | solution.py:23
  141.3 13.6 %collective-permute-start.8 = (f16[128,512]{1,0:T(8,128)(2,1)S(1)}, f16[128,512]{1,0:T(8,128)(2,1)S(1)}, u32[]{:S(2)}, u32[]{:S(2)}) collective-permute-start(f16[128,512]{1,0:T(8,128)(2,1)S(1)} %fusion.47), channel_id=1, source_target_pairs={{0,16},{4,20},{8,24},{12,28},{16,0},{20,4},{24,8},{28,12},{1,17},{... | collective-permute-start | bytes 393224 | tf_op jit(solution)/shard_map/ppermute | solution.py:23
  155.8 11.5 %collective-permute-start.13 = (f16[2,128,512]{2,1,0:T(8,128)(2,1)S(1)}, f16[2,128,512]{2,1,0:T(8,128)(2,1)S(1)}, u32[]{:S(2)}, u32[]{:S(2)}) collective-permute-start(f16[2,128,512]{2,1,0:T(8,128)(2,1)S(1)} %fusion.43), channel_id=1, source_target_pairs={{0,8},{4,12},{8,0},{12,4},{16,24},{20,28},{24,16},{28,20},{1,9},{5... | collective-permute-start | bytes 786440 | tf_op jit(solution)/shard_map/ppermute | solution.py:23
  161.0 16.4 %collective-permute-start.16 = (f16[2,128,512]{2,1,0:T(8,128)(2,1)}, f16[2,128,512]{2,1,0:T(8,128)(2,1)}, u32[]{:S(2)}, u32[]{:S(2)}) collective-permute-start(f16[2,128,512]{2,1,0:T(8,128)(2,1)} %fusion.40), channel_id=1, source_target_pairs={{0,16},{4,20},{8,24},{12,28},{16,0},{20,4},{24,8},{28,12},{1,17},{... | collective-permute-start | bytes 786440 | tf_op jit(solution)/shard_map/ppermute | solution.py:23
  178.8 13.2 %collective-permute-start.18 = (f16[2,2,128,512]{3,2,1,0:T(8,128)(2,1)S(1)}, f16[2,2,128,512]{3,2,1,0:T(8,128)(2,1)S(1)}, u32[]{:S(2)}, u32[]{:S(2)}) collective-permute-start(f16[2,2,128,512]{3,2,1,0:T(8,128)(2,1)S(1)} %fusion.32), channel_id=1, source_target_pairs={{0,4},{4,0},{8,12},{12,8},{16,20},{20,16},{24,28},{28,24},{1,5},{5... | collective-permute-start | bytes 1572872 | tf_op jit(solution)/shard_map/ppermute | solution.py:23
  180.9 15.6 %collective-permute-start.21 = (f16[2,2,128,512]{3,2,1,0:T(8,128)(2,1)S(1)}, f16[2,2,128,512]{3,2,1,0:T(8,128)(2,1)S(1)}, u32[]{:S(2)}, u32[]{:S(2)}) collective-permute-start(f16[2,2,128,512]{3,2,1,0:T(8,128)(2,1)S(1)} %fusion.33), channel_id=1, source_target_pairs={{0,8},{4,12},{8,0},{12,4},{16,24},{20,28},{24,16},{28,20},{1,9},{5... | collective-permute-start | bytes 1572872 | tf_op jit(solution)/shard_map/ppermute | solution.py:23
  196.8 14.4 %collective-permute-start.22 = (f16[2,128,512]{2,1,0:T(8,128)(2,1)S(1)}, f16[2,128,512]{2,1,0:T(8,128)(2,1)S(1)}, u32[]{:S(2)}, u32[]{:S(2)}) collective-permute-start(f16[2,128,512]{2,1,0:T(8,128)(2,1)S(1)} %fusion.41), channel_id=1, source_target_pairs={{0,16},{4,20},{8,24},{12,28},{16,0},{20,4},{24,8},{28,12},{1,17},{... | collective-permute-start | bytes 786440 | tf_op jit(solution)/shard_map/ppermute | solution.py:23
  201.0 11.5 %collective-permute-start.20 = (f16[128,512]{1,0:T(8,128)(2,1)S(1)}, f16[128,512]{1,0:T(8,128)(2,1)S(1)}, u32[]{:S(2)}, u32[]{:S(2)}) collective-permute-start(f16[128,512]{1,0:T(8,128)(2,1)S(1)} %fusion.51), channel_id=1, source_target_pairs={{0,16},{4,20},{8,24},{12,28},{16,0},{20,4},{24,8},{28,12},{1,17},{... | collective-permute-start | bytes 393224 | tf_op jit(solution)/shard_map/ppermute | solution.py:23
  (19 other events, 148.1 us)
Sparse Core Ops, SparseCore 0:
  18.1 37.1 all-gather.6
  56.9 34.4 all-gather.4
  93.0 34.4 all-gather.8
  129.5 34.4 all-gather.10
